TPU v7x, 32 devices: a whole 2x2x4 slice. The times are simulated.
32 devices in a mesh: ka: 4 (over x, core), brick: 8 (over z, y).
Axes of the slice: x: 2, y: 2, z: 4, core: 2. Of those that a mesh axis runs over, the one named last changes fastest.
Arguments:
- spinors: bfloat16 [32, 4, 32, 36864], P('ka', None, 'brick'), may hold values from -6 to 6
- kpt_mult: int32 [32], P('ka'), may hold values from 1 to 4
- occupied: int32 [32], P('ka'), may hold values 0 or 1
- core_density: float32 [32, 36864], P('brick'), may hold values from 0.05 to 1
- local_potential: float32 [32, 36864], P('brick'), may hold values from -6 to 6
Outputs:
- applied: bfloat16 [32, 4, 32, 36864], P('ka', None, 'brick')
All inputs are finite; a program needn't handle non-finite values. No bound on the sum of `occupied` on one device may be relied on, other than what follows from the above.
Results may differ from a plain program's by a relative error of at most 0.005.
Values may be sent and summed in bfloat16 or wider, within the bound.
No kernel may reach another device: no remote copies, remote signals or barrier semaphores. Data moves between devices by JAX's collectives and lax.ppermute only.
A program may use at most 128 MiB of HBM per device.

v0:
```python
import functools
import math

import jax
import jax.numpy as jnp
from jax import lax
from jax.experimental import pallas as pl
from jax.experimental.pallas import tpu as pltpu
from jax.sharding import PartitionSpec as P

NY = 192
LANES = 128
SUB = 8
TRIPLE = 3
HALF = 2 * NY - 2 * LANES - LANES // 2
PACK = 16
FLOOR_FRACTION = 0.05
VMEM_LIMIT = 63 * 1024 * 1024
SMALL = pl.CostEstimate(flops=0, bytes_accessed=0, transcendentals=0)


def rows_view(x):
    lead, planes, cells = x.shape[:-2], x.shape[-2], x.shape[-1]
    tiles = cells // LANES
    n = len(lead)
    x = x.reshape(lead + (planes, tiles, LANES))
    x = x.transpose(tuple(range(n)) + (n + 1, n, n + 2))
    return x.reshape(lead + (tiles * planes, LANES))


def planes_view(x, planes):
    lead, rows = x.shape[:-2], x.shape[-2]
    tiles = rows // planes
    n = len(lead)
    x = x.reshape(lead + (tiles, planes, LANES))
    x = x.transpose(tuple(range(n)) + (n + 1, n, n + 2))
    return x.reshape(lead + (planes, tiles * LANES))


def even_brick():
    return lax.axis_index("brick") % 2 == 0


def spread_matrix(back):
    size = SUB * PACK
    row = lax.broadcasted_iota(jnp.int32, (size, size), 0)
    column = lax.broadcasted_iota(jnp.int32, (size, size), 1)
    if back:
        row, column = column, row
    return (column == (row % SUB) * PACK + row // SUB).astype(jnp.bfloat16)


def gathered(read, segment, i):
    return jnp.concatenate(
        [read(pl.ds(s * segment + i * PACK, PACK)) for s in range(SUB)], axis=0
    )


def product(matrix, values):
    return jnp.dot(matrix, values, preferred_element_type=jnp.float32)


def face_matrix(planes):
    out = PACK // planes * SUB
    row = lax.broadcasted_iota(jnp.int32, (2 * out, SUB * PACK), 0)
    column = lax.broadcasted_iota(jnp.int32, (2 * out, SUB * PACK), 1)
    upper = (row < out) == even_brick()
    inner = row % out
    wanted = (inner % SUB) * PACK + (inner // SUB) * planes + jnp.where(upper, planes - 1, 0)
    return (column == wanted).astype(jnp.bfloat16), out


def edges_body(planes, chunks, x_ref, *refs):
    faces, held, sems = refs[-2 - 2 * len(chunks) : -2], refs[-2], refs[-1]
    first = chunks[0][0]
    bands = [(start - first + b, k, b) for k, (start, count) in enumerate(chunks) for b in range(count)]
    rows = held.shape[2]
    segment = rows // SUB
    copies = [pltpu.make_async_copy(x_ref.at[first + i], held.at[i], sems.at[i]) for i, _, _ in bands]
    for copy in copies:
        copy.start()
    select, out = face_matrix(planes)
    for i, k, b in bands:
        copies[i].wait()
        near_ref, far_ref = faces[2 * k], faces[2 * k + 1]
        for part in range(segment // PACK):
            block = jnp.concatenate(
                [gathered(lambda at: held[i, c, at, :], segment, part) for c in range(4)], axis=1
            )
            picked = product(select, block).astype(jnp.bfloat16)
            at = pl.ds(part * out, out)
            for c in range(4):
                lanes = slice(c * LANES, (c + 1) * LANES)
                near_ref[b, c, at, :] = picked[:out, lanes]
                far_ref[b, c, at, :] = picked[out:, lanes]


def edges(x, planes, chunks, after, limit):
    rows = x.shape[2]
    total = sum(count for _, count in chunks)
    shapes = [
        jax.ShapeDtypeStruct((count, 4, rows // planes, LANES), jnp.bfloat16) for _, count in chunks for _ in range(2)
    ]
    faces = pl.pallas_call(
        functools.partial(edges_body, planes, chunks),
        in_specs=[pl.BlockSpec(memory_space=pltpu.HBM)] + [pl.BlockSpec(memory_space=pl.ANY)] * len(after),
        out_shape=shapes,
        scratch_shapes=[pltpu.VMEM((total, 4, rows, LANES), jnp.bfloat16), pltpu.SemaphoreType.DMA((total,))],
        compiler_params=pltpu.CompilerParams(vmem_limit_bytes=limit),
        cost_estimate=SMALL,
        name="edges",
    )(x, *after)
    return [tuple(faces[2 * k : 2 * k + 2]) for k in range(len(chunks))]


def gate(near, far, after):
    anywhere = pl.BlockSpec(memory_space=pl.ANY)
    return pl.pallas_call(
        lambda *refs: None,
        in_specs=[anywhere] * (2 + len(after)),
        out_specs=[anywhere, anywhere],
        out_shape=[jax.ShapeDtypeStruct(a.shape, a.dtype) for a in (near, far)],
        input_output_aliases={0: 0, 1: 1},
        compiler_params=pltpu.CompilerParams(vmem_limit_bytes=VMEM_LIMIT),
        name="gate",
    )(near, far, *after)


def front_body(planes, scale, counts, mult_ref, occ_ref, x_ref, *refs):
    bands = x_ref.shape[0]
    first = len(refs) - 2 * len(counts)
    mine_ref, other_ref, faces = refs[first - 2], refs[first - 1], refs[first:]
    lower_half = holds_lower_half()
    weights = [(mult_ref[b] * occ_ref[b]).astype(jnp.float32) * scale for b in range(bands)]
    for s in range(SUB):
        up = down = real = imag = None
        for b in range(bands):
            ur, ui, dr, di = (x_ref[b, c, s].astype(jnp.float32) for c in range(4))
            wur, wui = weights[b] * ur, weights[b] * ui
            wdr, wdi = weights[b] * dr, weights[b] * di
            terms = (
                wur * ur + wui * ui,
                wdr * dr + wdi * di,
                wur * dr + wui * di,
                wur * di - wui * dr,
            )
            if b == 0:
                up, down, real, imag = terms
            else:
                up, down, real, imag = up + terms[0], down + terms[1], real + terms[2], imag + terms[3]
        fields = (up + down, 2.0 * real, 2.0 * imag, up - down)
        for f in range(2):
            mine_ref[f, s] = jnp.where(lower_half, fields[f], fields[f + 2]).astype(jnp.bfloat16)
            other_ref[f, s] = jnp.where(lower_half, fields[f + 2], fields[f]).astype(jnp.bfloat16)
    if counts:
        select, out = face_matrix(planes)
    band = bands - sum(counts)
    for k, count in enumerate(counts):
        for b in range(count):
            block = jnp.concatenate(
                [x_ref[band, c].reshape(SUB * PACK, LANES) for c in range(4)], axis=1
            )
            picked = product(select, block).astype(jnp.bfloat16)
            for c in range(4):
                lanes = slice(c * LANES, (c + 1) * LANES)
                faces[2 * k][b, c] = picked[:out, lanes]
                faces[2 * k + 1][b, c] = picked[out:, lanes]
            band += 1


def front(x, mult, occ, total, planes, counts, after):
    bands, rows = x.shape[0], x.shape[2]
    segment = rows // SUB
    out = PACK // planes * SUB
    anywhere = pl.BlockSpec(memory_space=pl.ANY)
    results = pl.pallas_call(
        functools.partial(front_body, planes, 1.0 / (2.0 * total), counts),
        grid=(segment // PACK,),
        in_specs=[
            pl.BlockSpec(memory_space=pltpu.SMEM),
            pl.BlockSpec(memory_space=pltpu.SMEM),
            pl.BlockSpec((bands, 4, SUB, PACK, LANES), lambda i: (0, 0, 0, i, 0)),
        ]
        + [anywhere] * len(after),
        out_specs=[pl.BlockSpec((2, SUB, PACK, LANES), lambda i: (0, 0, i, 0))] * 2
        + [pl.BlockSpec((count, 4, out, LANES), lambda i: (0, 0, i, 0)) for count in counts for _ in range(2)],
        out_shape=[jax.ShapeDtypeStruct((2, SUB, segment, LANES), jnp.bfloat16)] * 2
        + [
            jax.ShapeDtypeStruct((count, 4, rows // planes, LANES), jnp.bfloat16)
            for count in counts
            for _ in range(2)
        ],
        compiler_params=pltpu.CompilerParams(vmem_limit_bytes=VMEM_LIMIT),
        cost_estimate=SMALL,
        name="front",
    )(mult, occ, x.reshape(bands, 4, SUB, segment, LANES), *after)
    halves = [half.reshape(2, rows, LANES) for half in results[:2]]
    return halves, [tuple(results[2 + 2 * k : 4 + 2 * k]) for k in range(len(counts))]


def add_body(a_ref, b_ref, out_ref):
    out_ref[...] = (a_ref[...].astype(jnp.float32) + b_ref[...].astype(jnp.float32)).astype(jnp.bfloat16)


def add(a, b):
    whole = pl.BlockSpec(memory_space=pltpu.VMEM)
    return pl.pallas_call(
        add_body,
        in_specs=[whole, whole],
        out_specs=whole,
        out_shape=jax.ShapeDtypeStruct(a.shape, a.dtype),
        compiler_params=pltpu.CompilerParams(vmem_limit_bytes=VMEM_LIMIT),
        cost_estimate=SMALL,
        name="add",
    )(a, b)


def holds_lower_half():
    return lax.axis_index("ka") % 2 == 0


def group_sum(mine, other):
    size = lax.axis_size("ka")
    assert size % 2 == 0
    partner = [(i, i ^ 1) for i in range(size)]

    def swaps(_, fields):
        total, given = fields
        total = add(total, lax.ppermute(given, "ka", partner))
        turning = total
        for _ in range(size // 2 - 1):
            turning = lax.ppermute(turning, "ka", [(i, (i + 2) % size) for i in range(size)])
            total = add(total, turning)
        return total, lax.ppermute(total, "ka", partner)

    trips = 1 + lax.div(lax.axis_index("ka"), size)
    return lax.fori_loop(0, trips, swaps, (mine, other))


def cube_root(x):
    root = jnp.exp(jnp.log(jnp.abs(x)) * (1.0 / 3.0))
    return jnp.where(x < 0.0, -root, root)


def potential_body(rows, mine_ref, other_ref, core_ref, local_ref, out_ref):
    segment = rows // SUB
    spread = spread_matrix(False)

    lower_half = holds_lower_half()

    def step(i, unused):
        block = jnp.concatenate(
            [gathered(lambda at: ref[f, at, :], segment, i) for ref in (mine_ref, other_ref) for f in range(2)], axis=1
        )
        fields = product(spread, block)
        m0, m1, o0, o1 = (fields[:, f * LANES : (f + 1) * LANES] for f in range(4))
        d0, d1 = jnp.where(lower_half, m0, o0), jnp.where(lower_half, m1, o1)
        d2, d3 = jnp.where(lower_half, o0, m0), jnp.where(lower_half, o1, m1)
        here = [pl.ds(i * PACK + r, SUB, stride=segment) for r in range(PACK)]
        core = jnp.concatenate([core_ref[at, :] for at in here], axis=0)
        local = jnp.concatenate([local_ref[at, :] for at in here], axis=0)
        electrons = d0 + core
        magnitude = jnp.sqrt(d1 * d1 + d2 * d2 + d3 * d3)
        upper = -cube_root((3.0 / math.pi) * (electrons + magnitude))
        lower = -cube_root((3.0 / math.pi) * (electrons - magnitude))
        factor = 0.5 * (upper - lower) / jnp.maximum(magnitude, FLOOR_FRACTION * electrons)
        v = 0.5 * (upper + lower) + local
        bz = factor * d3
        at = pl.ds(i * PACK, PACK)
        shape = (PACK, SUB, LANES)
        out_ref[0, at] = (v + bz + 3.0).reshape(shape)
        out_ref[1, at] = (factor * d1).reshape(shape)
        out_ref[2, at] = (factor * d2).reshape(shape)
        out_ref[3, at] = (v - bz + 3.0).reshape(shape)
        return unused

    lax.fori_loop(0, segment // PACK, step, 0, unroll=True)


def potential_of(mine, other, core, local):
    rows = mine.shape[1]
    whole = pl.BlockSpec(memory_space=pltpu.VMEM)
    return pl.pallas_call(
        functools.partial(potential_body, rows),
        in_specs=[whole, whole, whole, whole],
        out_specs=whole,
        out_shape=jax.ShapeDtypeStruct((4, rows // SUB, SUB, LANES), jnp.float32),
        compiler_params=pltpu.CompilerParams(vmem_limit_bytes=VMEM_LIMIT),
        cost_estimate=SMALL,
        name="potential",
    )(mine, other, core, local)


def apply_body(planes, rows, x_ref, pot_ref, near_ref, far_ref, carry_ref, out_ref, token_ref, wide, ends, turned, flat):
    segment = rows // SUB
    stride = planes * TRIPLE
    steps = segment // stride
    near_slot = jnp.where(even_brick(), 1, 0)
    spread, unspread = spread_matrix(False), spread_matrix(True)

    for c in range(4):
        ends[near_slot, c] = near_ref[0, c].astype(jnp.float32).reshape(ends.shape[2:])
        ends[1 - near_slot, c] = far_ref[0, c].astype(jnp.float32).reshape(ends.shape[2:])

    def load(i, unused):
        block = jnp.concatenate([gathered(lambda at: x_ref[0, c, at, :], segment, i) for c in range(4)], axis=1)
        values = product(spread, block)
        for c in range(4):
            part = values[:, c * LANES : (c + 1) * LANES]
            wide[c, pl.ds(i * PACK, PACK)] = part.reshape(PACK, SUB, LANES)
            turned[c, pl.ds(stride + i * PACK, PACK)] = pltpu.roll(part, HALF, 1).reshape(PACK, SUB, LANES)
        return unused

    lax.fori_loop(0, segment // PACK, load, 0, unroll=True)
    for c in range(4):
        for q in range(stride):
            turned[c, q] = pltpu.roll(turned[c, segment + q], 1, 0)
            turned[c, segment + stride + q] = pltpu.roll(turned[c, stride + q], SUB - 1, 0)

    lane = lax.broadcasted_iota(jnp.int32, (SUB, LANES), 1)
    low = lane < HALF
    initial, final = lane == 0, lane == LANES - 1
    inner_initial, inner_final = lane == HALF, lane == HALF - 1

    def neighbours(c, plane, j):
        spot = [j * stride + tile * planes + plane for tile in range(TRIPLE)]
        v0, v1, v2 = (wide[c, at] for at in spot)
        r0, r1, r2 = (turned[c, at + stride] for at in spot)
        after0 = r0 + turned[c, spot[0] + 2 * stride]
        after1 = r1 + turned[c, spot[1] + 2 * stride]
        before1 = r1 + turned[c, spot[1]]
        before2 = r2 + turned[c, spot[2]]
        across = (
            jnp.where(low, before1, before2),
            jnp.where(low, before2, after0),
            jnp.where(low, after0, after1),
        )
        plus = (
            jnp.where(initial, v1, v0),
            jnp.where(inner_initial, r0, jnp.where(initial, v2, v1)),
            jnp.where(initial, r1, v2),
        )
        minus = (
            jnp.where(final, r1, v0),
            jnp.where(inner_final, r2, jnp.where(final, v0, v1)),
            jnp.where(final, v1, v2),
        )
        sums = []
        for tile in range(TRIPLE):
            below = ends[0, c, j * TRIPLE + tile] if plane == 0 else wide[c, spot[tile] - 1]
            above = ends[1, c, j * TRIPLE + tile] if plane == planes - 1 else wide[c, spot[tile] + 1]
            along = pltpu.roll(plus[tile], LANES - 1, 1) + pltpu.roll(minus[tile], 1, 1)
            sums.append((across[tile] + along) + (below + above))
        return (v0, v1, v2), sums

    def step(j, unused):
        for plane in range(planes):
            (ur, nur), (ui, nui), (dr, ndr), (di, ndi) = (neighbours(c, plane, j) for c in range(4))
            for tile in range(TRIPLE):
                spot = j * stride + tile * planes + plane
                diag_up, bx, by, diag_down = (pot_ref[f, spot] for f in range(4))
                a, b, e, f = ur[tile], ui[tile], dr[tile], di[tile]
                flat[0, spot] = diag_up * a + bx * e + by * f - 0.5 * nur[tile]
                flat[1, spot] = diag_up * b + bx * f - by * e - 0.5 * nui[tile]
                flat[2, spot] = bx * a - by * b + diag_down * e - 0.5 * ndr[tile]
                flat[3, spot] = bx * b + by * a + diag_down * f - 0.5 * ndi[tile]
        return unused

    lax.fori_loop(0, steps, step, 0)

    def store(i, unused):
        at = pl.ds(i * PACK, PACK)
        block = jnp.concatenate([flat[c, at].reshape(PACK * SUB, LANES) for c in range(4)], axis=1)
        values = product(unspread, block.astype(jnp.bfloat16)).astype(jnp.bfloat16)
        for c in range(4):
            for s in range(SUB):
                out_ref[0, c, pl.ds(pl.multiple_of(s * segment + i * PACK, PACK), PACK), :] = values[
                    s * PACK : (s + 1) * PACK, c * LANES : (c + 1) * LANES
                ]
        return unused

    lax.fori_loop(0, segment // PACK, store, 0, unroll=True)


def apply_bands(x, potential, near, far, planes, start, carry):
    count, rows = near.shape[0], x.shape[2]
    segment = rows // SUB
    stride = planes * TRIPLE
    tiles = rows // planes
    halo = pl.BlockSpec((1, 4, tiles, LANES), lambda b: (b, 0, 0, 0))
    body = functools.partial(apply_body, planes, rows)
    in_specs = [
        pl.BlockSpec((1, 4, rows, LANES), lambda b: (start + b, 0, 0, 0)),
        pl.BlockSpec((4, segment, SUB, LANES), lambda b: (0, 0, 0, 0)),
        halo,
        halo,
    ]
    operands = [x, potential, near, far]
    aliases = {}
    if carry is not None:
        in_specs.append(pl.BlockSpec(memory_space=pl.ANY))
        operands.append(carry)
        aliases = {4: 0}
        call = body
    else:

        def call(x_ref, pot_ref, near_ref, far_ref, *rest):
            body(x_ref, pot_ref, near_ref, far_ref, None, *rest)

    return pl.pallas_call(
        call,
        grid=(count,),
        in_specs=in_specs,
        out_specs=[
            pl.BlockSpec((1, 4, rows, LANES), lambda b: (start + b, 0, 0, 0)),
            pl.BlockSpec(memory_space=pl.ANY),
        ],
        out_shape=[
            jax.ShapeDtypeStruct(x.shape, jnp.bfloat16),
            jax.ShapeDtypeStruct((SUB, LANES), jnp.float32),
        ],
        input_output_aliases=aliases,
        scratch_shapes=[
            pltpu.VMEM((4, segment, SUB, LANES), jnp.float32),
            pltpu.VMEM((2, 4, tiles // SUB, SUB, LANES), jnp.float32),
            pltpu.VMEM((4, segment + 2 * stride, SUB, LANES), jnp.float32),
            pltpu.VMEM((4, segment, SUB, LANES), jnp.float32),
        ],
        compiler_params=pltpu.CompilerParams(vmem_limit_bytes=VMEM_LIMIT),
        cost_estimate=SMALL,
        name="apply",
    )(*operands)


def chunk_sizes(bands):
    ends = max(bands // 4, 1)
    return [n for n in (ends, bands - 2 * ends, ends) if n > 0] if bands > 1 else [1]


def shards(spinors, kpt_mult, occupied, core_density, local_potential):
    bands, planes = spinors.shape[0], spinors.shape[2]
    total = bands * lax.axis_size("ka")
    size = lax.axis_size("brick")
    near_pairs = [(i, i ^ 1) for i in range(size) if i ^ 1 < size]
    far_pairs = [(i, j) for i in range(size) for j in [((i + 1) ^ 1) - 1] if 0 <= j < size]
    x = rows_view(spinors)
    core, local = rows_view(core_density), rows_view(local_potential)
    sizes = chunk_sizes(bands)
    starts = [sum(sizes[:k]) for k in range(len(sizes))]

    swap = lambda face: (lax.ppermute(face[0], "brick", near_pairs), lax.ppermute(face[1], "brick", far_pairs))
    faces = edges(x, planes, [(0, sizes[0])], (), VMEM_LIMIT)
    halos = [swap(faces[0])]
    density, others = front(x, kpt_mult, occupied, total, planes, sizes[1:], faces[0])
    faces += others
    halos += [swap(face) for face in faces[1:2]]
    potential = potential_of(*group_sum(*density), core, local)
    out, token = None, (potential,)
    for k, start in enumerate(starts):
        if k + 2 < len(starts):
            halos.append(swap(gate(*faces[k + 2], halos[k] + token)))
        out, done = apply_bands(x, potential, *halos[k], planes, start, out)
        token = (done,)
    return planes_view(out, planes)


def solution(mesh):
    placed = (P("ka", None, "brick", None), P("ka"), P("ka"), P("brick", None), P("brick", None))
    return jax.shard_map(
        shards, mesh=mesh, in_specs=placed, out_specs=P("ka", None, "brick", None), check_vma=False
    )
```

profile of v0, /device:TPU:0, one launch (start us, length us, event | category | flops | bytes accessed | tf_op | source)
XLA Modules:
  0.0 124.5 jit_solution(12749807099591580221)
XLA Ops:
  0.0 3.0 %edges.1 = (bf16[2,4,288,128]{3,2,1,0:T(8,128)(2,1)}, bf16[2,4,288,128]{3,2,1,0:T(8,128)(2,1)}) custom-call(bf16[8,4,1152,128]{3,2,1,0:T(8,128)(2,1)} %bitcast.24), custom_call_target="tpu_custom_call" | custom-call | tf_op jit(solution)/shard_map/edges/pallas_call | solution.py:104
  3.0 3.0 %collective-permute-start.3 = (bf16[2,4,288,128]{3,2,1,0:T(8,128)(2,1)}, bf16[2,4,288,128]{3,2,1,0:T(8,128)(2,1)}, u32[]{:S(2)}, u32[]{:S(2)}) collective-permute-start(bf16[2,4,288,128]{3,2,1,0:T(8,128)(2,1)} %get-tuple-element.42.refs_0_), channel_id=1, source_target_pairs={{0,1},{1,0},{2,3},{3,2},{4,5},{5,4},{6,7},{7,6},{8,9},{9,8},{10,11... | collective-permute-start | bytes 1769480 | tf_op jit(solution)/shard_map/ppermute | solution.py:451
  6.0 1.5 %collective-permute-start.4 = (bf16[2,4,288,128]{3,2,1,0:T(8,128)(2,1)}, bf16[2,4,288,128]{3,2,1,0:T(8,128)(2,1)}, u32[]{:S(2)}, u32[]{:S(2)}) collective-permute-start(bf16[2,4,288,128]{3,2,1,0:T(8,128)(2,1)} %get-tuple-element.43.refs_1_), channel_id=1, source_target_pairs={{1,2},{2,1},{3,4},{4,3},{5,6},{6,5},{9,10},{10,9},{11,12},{12,11},... | collective-permute-start | bytes 1769480 | tf_op jit(solution)/shard_map/ppermute | solution.py:451
  7.6 11.0 %front.1 = (bf16[2,8,144,128]{3,2,1,0:T(8,128)(2,1)S(1)}, bf16[2,8,144,128]{3,2,1,0:T(8,128)(2,1)}, bf16[4,4,288,128]{3,2,1,0:T(8,128)(2,1)}, bf16[4,4,288,128]{...) custom-call(s32[8]{0:T(128)} %mult_ref.1, s32[8]{0:T(128)} %occ_ref.1, ...), custom_call_target="tpu_custom_call" | custom-call | tf_op jit(solution)/shard_map/front/pallas_call | solution.py:176
  18.5 3.4 %collective-permute-start.7 = (bf16[4,4,288,128]{3,2,1,0:T(8,128)(2,1)}, bf16[4,4,288,128]{3,2,1,0:T(8,128)(2,1)}, u32[]{:S(2)}, u32[]{:S(2)}) collective-permute-start(bf16[4,4,288,128]{3,2,1,0:T(8,128)(2,1)} %get-tuple-element.52), channel_id=1, source_target_pairs={{0,1},{1,0},{2,3},{3,2},{4,5},{5,4},{6,7},{7,6},{8,9},{9,8},{10,11... | collective-permute-start | bytes 3538952 | tf_op jit(solution)/shard_map/ppermute | solution.py:451
  22.0 1.7 %collective-permute-start.8 = (bf16[4,4,288,128]{3,2,1,0:T(8,128)(2,1)}, bf16[4,4,288,128]{3,2,1,0:T(8,128)(2,1)}, u32[]{:S(2)}, u32[]{:S(2)}) collective-permute-start(bf16[4,4,288,128]{3,2,1,0:T(8,128)(2,1)} %get-tuple-element.53), channel_id=1, source_target_pairs={{1,2},{2,1},{3,4},{4,3},{5,6},{6,5},{9,10},{10,9},{11,12},{12,11},... | collective-permute-start | bytes 3538952 | tf_op jit(solution)/shard_map/ppermute | solution.py:451
  23.7 24.3 %while.12 = (s32[]{:T(128)}, bf16[2,1152,128]{2,1,0:T(8,128)(2,1)S(1)}, bf16[2,1152,128]{2,1,0:T(8,128)(2,1)}, s32[]{:T(128)}, s32[]{:T(128)}) while((s32[]{:T(128)}, bf16[2,1152,128]{2,1,0:T(8,128)(2,1)S(1)}, bf16[2,1152,128]{2,1,0:T(8,128)(2,1)}, s32[]{:T(128)}, s32[]{:T(128)}) %tuple.22), condition=%wide.region_1.0_spmd, body=%wide.region_0.0_spmd.sunk | while | flops 2 | bytes 9437393 | solution.py:237
  23.7 2.3 %collective-permute-done.b_ref = bf16[2,1152,128]{2,1,0:T(8,128)(2,1)} collective-permute-done((bf16[2,1152,128]{2,1,0:T(8,128)(2,1)}, bf16[2,1152,128]{2,1,0:T(8,128)(2,1)}, u32[]{:S(2)}, u32[]{:S(2)}) %collective-permute-start) | collective-permute-done | bytes 589856 | tf_op jit(solution)/shard_map/while/body/ppermute | solution.py:229
  26.0 2.0 %add.11.a_ref = bf16[2,1152,128]{2,1,0:T(8,128)(2,1)} custom-call(bf16[2,1152,128]{2,1,0:T(8,128)(2,1)S(1)} %get-tuple-element.97.a_ref, bf16[2,1152,128]{2,1,0:T(8,128)(2,1)} %collective-permute-done.b_ref), custom_call_target="tpu_custom_call" | custom-call | tf_op jit(solution)/shard_map/while/body/add/pallas_call | solution.py:207
  28.0 1.5 %collective-permute-start.1 = (bf16[2,1152,128]{2,1,0:T(8,128)(2,1)}, bf16[2,1152,128]{2,1,0:T(8,128)(2,1)}, u32[]{:S(2)}, u32[]{:S(2)}) collective-permute-start(bf16[2,1152,128]{2,1,0:T(8,128)(2,1)} %add.11.a_ref), channel_id=1, source_target_pairs={{0,16},{8,24},{16,0},{24,8},{1,17},{9,25},{17,1},{25,9},{2,18},{10... | collective-permute-start | bytes 1769480 | tf_op jit(solution)/shard_map/while/body/ppermute | solution.py:232
  29.5 14.2 %collective-permute-done.1.b_ref = bf16[2,1152,128]{2,1,0:T(8,128)(2,1)} collective-permute-done((bf16[2,1152,128]{2,1,0:T(8,128)(2,1)}, bf16[2,1152,128]{2,1,0:T(8,128)(2,1)}, u32[]{:S(2)}, u32[]{:S(2)}) %collective-permute-start.1) | collective-permute-done | bytes 589856 | tf_op jit(solution)/shard_map/while/body/ppermute | solution.py:232
  43.7 1.4 %add.12 = bf16[2,1152,128]{2,1,0:T(8,128)(2,1)S(1)} custom-call(bf16[2,1152,128]{2,1,0:T(8,128)(2,1)} %add.11.a_ref, bf16[2,1152,128]{2,1,0:T(8,128)(2,1)} %collective-permute-done.1.b_ref), custom_call_target="tpu_custom_call" | custom-call | tf_op jit(solution)/shard_map/while/body/add/pallas_call | solution.py:207
  45.1 0.1 collective-permute-start.2
  45.2 2.0 %collective-permute-done.2 = bf16[2,1152,128]{2,1,0:T(8,128)(2,1)S(1)} collective-permute-done((bf16[2,1152,128]{2,1,0:T(8,128)(2,1)S(1)}, bf16[2,1152,128]{2,1,0:T(8,128)(2,1)S(1)}, u32[]{:S(2)}, u32[]{:S(2)}) %collective-permute-start.2) | collective-permute-done | bytes 589856 | tf_op jit(solution)/shard_map/while/body/ppermute | solution.py:234
  47.2 0.8 copy-done
  48.0 4.3 %potential.1.refs_4_.pot_ref = f32[4,144,8,128]{3,2,1,0:T(8,128)} custom-call(bf16[2,1152,128]{2,1,0:T(8,128)(2,1)S(1)} %get-tuple-element.46.mine_ref, bf16[2,1152,128]{2,1,0:T(8,128)(2,1)} %get-tuple-element.47.other_ref, f32[1152,128]{1,0:T(8,128)} %bitcast.30, f32[1152,128]{1,0:T(8,128)} %bitcast.31), custom_call_target="tpu_custom_call" | custom-call | tf_op jit(solution)/shard_map/potential/pallas_call | solution.py:283
  52.3 5.7 %collective-permute-done.3.refs_2_.near_ref = bf16[2,4,288,128]{3,2,1,0:T(8,128)(2,1)} collective-permute-done((bf16[2,4,288,128]{3,2,1,0:T(8,128)(2,1)}, bf16[2,4,288,128]{3,2,1,0:T(8,128)(2,1)}, u32[]{:S(2)}, u32[]{:S(2)}) %collective-permute-start.3) | collective-permute-done | bytes 589856 | tf_op jit(solution)/shard_map/ppermute | solution.py:451
  58.0 2.5 %collective-permute-start.5 = (bf16[2,4,288,128]{3,2,1,0:T(8,128)(2,1)}, bf16[2,4,288,128]{3,2,1,0:T(8,128)(2,1)S(1)}, u32[]{:S(2)}, u32[]{:S(2)}) collective-permute-start(bf16[2,4,288,128]{3,2,1,0:T(8,128)(2,1)} %get-tuple-element.50), channel_id=1, source_target_pairs={{0,1},{1,0},{2,3},{3,2},{4,5},{5,4},{6,7},{7,6},{8,9},{9,8},{10,11... | collective-permute-start | bytes 1769480 | tf_op jit(solution)/shard_map/ppermute | solution.py:451
  60.5 1.5 %collective-permute-start.6 = (bf16[2,4,288,128]{3,2,1,0:T(8,128)(2,1)}, bf16[2,4,288,128]{3,2,1,0:T(8,128)(2,1)}, u32[]{:S(2)}, u32[]{:S(2)}) collective-permute-start(bf16[2,4,288,128]{3,2,1,0:T(8,128)(2,1)} %get-tuple-element.51), channel_id=1, source_target_pairs={{1,2},{2,1},{3,4},{4,3},{5,6},{6,5},{9,10},{10,9},{11,12},{12,11},... | collective-permute-start | bytes 1769480 | tf_op jit(solution)/shard_map/ppermute | solution.py:451
  62.0 10.3 %apply.3 = (bf16[8,4,1152,128]{3,2,1,0:T(8,128)(2,1)}, f32[8,128]{1,0:T(8,128)}) custom-call(bf16[8,4,1152,128]{3,2,1,0:T(8,128)(2,1)} %bitcast.26, f32[4,144,8,128]{3,2,1,0:T(8,128)} %potential.1.refs_4_.pot_ref, bf16[2,4,288,128]{3,2,1,0:T(8,128)(2,1)} %collective-permute-done.3.refs_2_.near_ref, ...), custom_call_target="tpu_custom_call" | custom-call | tf_op jit(solution)/shard_map/apply/pallas_call | solution.py:410
  72.3 23.6 %collective-permute-done.7.near_ref = bf16[4,4,288,128]{3,2,1,0:T(8,128)(2,1)} collective-permute-done((bf16[4,4,288,128]{3,2,1,0:T(8,128)(2,1)}, bf16[4,4,288,128]{3,2,1,0:T(8,128)(2,1)}, u32[]{:S(2)}, u32[]{:S(2)}) %collective-permute-start.7) | collective-permute-done | bytes 1179680 | tf_op jit(solution)/shard_map/ppermute | solution.py:451
  95.9 17.4 %apply.4 = (bf16[8,4,1152,128]{3,2,1,0:T(8,128)(2,1)}, f32[8,128]{1,0:T(8,128)}) custom-call(bf16[8,4,1152,128]{3,2,1,0:T(8,128)(2,1)} %bitcast.27, f32[4,144,8,128]{3,2,1,0:T(8,128)} %potential.1.refs_4_.pot_ref, bf16[4,4,288,128]{3,2,1,0:T(8,128)(2,1)} %collective-permute-done.7.near_ref, ...), custom_call_target="tpu_custom_call", output_to_operand_aliasing={{0}: (4, {})} | custom-call | tf_op jit(solution)/shard_map/apply/pallas_call | solution.py:410
  113.4 0.8 copy-done.1
  114.2 10.3 %apply.5 = (bf16[8,4,1152,128]{3,2,1,0:T(8,128)(2,1)}, f32[8,128]{1,0:T(8,128)}) custom-call(bf16[8,4,1152,128]{3,2,1,0:T(8,128)(2,1)} %bitcast.28, f32[4,144,8,128]{3,2,1,0:T(8,128)} %potential.1.refs_4_.pot_ref, bf16[2,4,288,128]{3,2,1,0:T(8,128)(2,1)} %copy-done.1, ...), custom_call_target="tpu_custom_call", output_to_operand_aliasing={{0}: (4, {})} | custom-call | tf_op jit(solution)/shard_map/apply/pallas_call | solution.py:410
  (8 shorter events, 0.0 us)
Async XLA Ops:
  3.0 55.0 %collective-permute-start.3 = (bf16[2,4,288,128]{3,2,1,0:T(8,128)(2,1)}, bf16[2,4,288,128]{3,2,1,0:T(8,128)(2,1)}, u32[]{:S(2)}, u32[]{:S(2)}) collective-permute-start(bf16[2,4,288,128]{3,2,1,0:T(8,128)(2,1)} %get-tuple-element.42.refs_0_), channel_id=1, source_target_pairs={{0,1},{1,0},{2,3},{3,2},{4,5},{5,4},{6,7},{7,6},{8,9},{9,8},{10,11... | collective-permute-start | bytes 1769480 | tf_op jit(solution)/shard_map/ppermute | solution.py:451
  6.0 52.0 %collective-permute-start.4 = (bf16[2,4,288,128]{3,2,1,0:T(8,128)(2,1)}, bf16[2,4,288,128]{3,2,1,0:T(8,128)(2,1)}, u32[]{:S(2)}, u32[]{:S(2)}) collective-permute-start(bf16[2,4,288,128]{3,2,1,0:T(8,128)(2,1)} %get-tuple-element.43.refs_1_), channel_id=1, source_target_pairs={{1,2},{2,1},{3,4},{4,3},{5,6},{6,5},{9,10},{10,9},{11,12},{12,11},... | collective-permute-start | bytes 1769480 | tf_op jit(solution)/shard_map/ppermute | solution.py:451
  18.5 77.4 %collective-permute-start.7 = (bf16[4,4,288,128]{3,2,1,0:T(8,128)(2,1)}, bf16[4,4,288,128]{3,2,1,0:T(8,128)(2,1)}, u32[]{:S(2)}, u32[]{:S(2)}) collective-permute-start(bf16[4,4,288,128]{3,2,1,0:T(8,128)(2,1)} %get-tuple-element.52), channel_id=1, source_target_pairs={{0,1},{1,0},{2,3},{3,2},{4,5},{5,4},{6,7},{7,6},{8,9},{9,8},{10,11... | collective-permute-start | bytes 3538952 | tf_op jit(solution)/shard_map/ppermute | solution.py:451
  22.0 73.9 %collective-permute-start.8 = (bf16[4,4,288,128]{3,2,1,0:T(8,128)(2,1)}, bf16[4,4,288,128]{3,2,1,0:T(8,128)(2,1)}, u32[]{:S(2)}, u32[]{:S(2)}) collective-permute-start(bf16[4,4,288,128]{3,2,1,0:T(8,128)(2,1)} %get-tuple-element.53), channel_id=1, source_target_pairs={{1,2},{2,1},{3,4},{4,3},{5,6},{6,5},{9,10},{10,9},{11,12},{12,11},... | collective-permute-start | bytes 3538952 | tf_op jit(solution)/shard_map/ppermute | solution.py:451
  23.7 2.3 %collective-permute-start = (bf16[2,1152,128]{2,1,0:T(8,128)(2,1)}, bf16[2,1152,128]{2,1,0:T(8,128)(2,1)}, u32[]{:S(2)}, u32[]{:S(2)}) collective-permute-start(bf16[2,1152,128]{2,1,0:T(8,128)(2,1)} %get-tuple-element.98), channel_id=1, source_target_pairs={{0,8},{8,0},{16,24},{24,16},{1,9},{9,1},{17,25},{25,17},{2,10},{10... | collective-permute-start | bytes 1769480 | tf_op jit(solution)/shard_map/while/body/ppermute | solution.py:229
  28.0 15.7 %collective-permute-start.1 = (bf16[2,1152,128]{2,1,0:T(8,128)(2,1)}, bf16[2,1152,128]{2,1,0:T(8,128)(2,1)}, u32[]{:S(2)}, u32[]{:S(2)}) collective-permute-start(bf16[2,1152,128]{2,1,0:T(8,128)(2,1)} %add.11.a_ref), channel_id=1, source_target_pairs={{0,16},{8,24},{16,0},{24,8},{1,17},{9,25},{17,1},{25,9},{2,18},{10... | collective-permute-start | bytes 1769480 | tf_op jit(solution)/shard_map/while/body/ppermute | solution.py:232
  45.1 2.1 %collective-permute-start.2 = (bf16[2,1152,128]{2,1,0:T(8,128)(2,1)S(1)}, bf16[2,1152,128]{2,1,0:T(8,128)(2,1)S(1)}, u32[]{:S(2)}, u32[]{:S(2)}) collective-permute-start(bf16[2,1152,128]{2,1,0:T(8,128)(2,1)S(1)} %add.12), channel_id=1, source_target_pairs={{0,8},{8,0},{16,24},{24,16},{1,9},{9,1},{17,25},{25,17},{2,10},{10... | collective-permute-start | bytes 1769480 | tf_op jit(solution)/shard_map/while/body/ppermute | solution.py:234
  47.2 0.8 copy-start
  58.0 55.3 %collective-permute-start.5 = (bf16[2,4,288,128]{3,2,1,0:T(8,128)(2,1)}, bf16[2,4,288,128]{3,2,1,0:T(8,128)(2,1)S(1)}, u32[]{:S(2)}, u32[]{:S(2)}) collective-permute-start(bf16[2,4,288,128]{3,2,1,0:T(8,128)(2,1)} %get-tuple-element.50), channel_id=1, source_target_pairs={{0,1},{1,0},{2,3},{3,2},{4,5},{5,4},{6,7},{7,6},{8,9},{9,8},{10,11... | collective-permute-start | bytes 1769480 | tf_op jit(solution)/shard_map/ppermute | solution.py:451
  60.5 52.9 %collective-permute-start.6 = (bf16[2,4,288,128]{3,2,1,0:T(8,128)(2,1)}, bf16[2,4,288,128]{3,2,1,0:T(8,128)(2,1)}, u32[]{:S(2)}, u32[]{:S(2)}) collective-permute-start(bf16[2,4,288,128]{3,2,1,0:T(8,128)(2,1)} %get-tuple-element.51), channel_id=1, source_target_pairs={{1,2},{2,1},{3,4},{4,3},{5,6},{6,5},{9,10},{10,9},{11,12},{12,11},... | collective-permute-start | bytes 1769480 | tf_op jit(solution)/shard_map/ppermute | solution.py:451
  113.3 0.8 copy-start.1
where the time goes:
time: 125 us
  Pallas kernels  59.8 us (48%)
  waiting for transfers between devices  47.8 us (38%)
  starting transfers between devices  15.2 us (12%)
  local copies, waits for them, and re-layouts  1.66 us (1%)
    pallas_call x3, Pallas kernels, apply_bands(): pl.pallas_call(call, grid=(count,), in_specs=in_specs, out_specs=[pl.Bloc...  38.1 us
    ppermute x3, waiting for transfers between devices, shards(): lax.ppermute(face[0], 'brick', near_pairs)  29.3 us
    ppermute x1, waiting for transfers between devices, swaps(): lax.ppermute(turning, 'ka', [(i, (i + 2) % size) for i in range(size)])  14.2 us
    pallas_call x1, Pallas kernels, front(): pl.pallas_call(functools.partial(front_body, planes, 1.0 / (2.0 * total),...  11 us
    ppermute x3, starting transfers between devices, shards(): lax.ppermute(face[0], 'brick', near_pairs)  8.95 us
    ppermute x3, starting transfers between devices, shards(): lax.ppermute(face[1], 'brick', far_pairs)  4.71 us
    pallas_call x1, Pallas kernels, potential_of(): pl.pallas_call(functools.partial(potential_body, rows), in_specs=[whole,...  4.33 us
    pallas_call x2, Pallas kernels, add(): pl.pallas_call(add_body, in_specs=[whole, whole], out_specs=whole, out_sh...  3.4 us
  transfers between devices with their start and end apart: 9, of which 5 were waited for; matrix products, arithmetic and copies ran while one was open for 0% of the time, Pallas kernels for 37%

commit v1 on v0

--- a/solution.py
+++ b/solution.py
@@ -242,7 +242,8 @@
     return jnp.where(x < 0.0, -root, root)
 
 
-def potential_body(rows, mine_ref, other_ref, core_ref, local_ref, out_ref):
+def potential_body(rows, mine_ref, other_ref, core_ref, local_ref, *refs):
+    out_ref = refs[-1]
     segment = rows // SUB
     spread = spread_matrix(False)
 
@@ -277,18 +278,18 @@
     lax.fori_loop(0, segment // PACK, step, 0, unroll=True)
 
 
-def potential_of(mine, other, core, local):
+def potential_of(mine, other, core, local, after):
     rows = mine.shape[1]
     whole = pl.BlockSpec(memory_space=pltpu.VMEM)
     return pl.pallas_call(
         functools.partial(potential_body, rows),
-        in_specs=[whole, whole, whole, whole],
+        in_specs=[whole] * 4 + [pl.BlockSpec(memory_space=pl.ANY)] * len(after),
         out_specs=whole,
         out_shape=jax.ShapeDtypeStruct((4, rows // SUB, SUB, LANES), jnp.float32),
         compiler_params=pltpu.CompilerParams(vmem_limit_bytes=VMEM_LIMIT),
         cost_estimate=SMALL,
         name="potential",
-    )(mine, other, core, local)
+    )(mine, other, core, local, *after)
 
 
 def apply_body(planes, rows, x_ref, pot_ref, near_ref, far_ref, carry_ref, out_ref, token_ref, wide, ends, turned, flat):
@@ -433,8 +434,7 @@
 
 
 def chunk_sizes(bands):
-    ends = max(bands // 4, 1)
-    return [n for n in (ends, bands - 2 * ends, ends) if n > 0] if bands > 1 else [1]
+    return [2] * (bands // 2) + [1] * (bands % 2)
 
 
 def shards(spinors, kpt_mult, occupied, core_density, local_potential):
@@ -454,10 +454,15 @@
     density, others = front(x, kpt_mult, occupied, total, planes, sizes[1:], faces[0])
     faces += others
     halos += [swap(face) for face in faces[1:2]]
-    potential = potential_of(*group_sum(*density), core, local)
-    out, token = None, (potential,)
+    density = group_sum(*density)
+    gated = ()
+    if len(starts) > 2:
+        gated = gate(*faces[2], halos[0] + (density[0],))
+        halos.append(swap(gated))
+    potential = potential_of(*density, core, local, gated)
+    out, token = None, ()
     for k, start in enumerate(starts):
-        if k + 2 < len(starts):
+        if 0 < k < len(starts) - 2:
             halos.append(swap(gate(*faces[k + 2], halos[k] + token)))
         out, done = apply_bands(x, potential, *halos[k], planes, start, out)
         token = (done,)

time: 125 us -> 119 us (0.952)
  waiting for transfers between devices: 47.8 us -> 33.3 us
  starting transfers between devices: 15.2 us -> 20.1 us
  Pallas kernels: 59.8 us -> 63.5 us
    ppermute x3 -> x4, waiting for transfers between devices: 29.3 us -> 14.7 us  [shards(): lax.ppermute(face[0], 'brick', near_pairs)]
    ppermute x3 -> x4, starting transfers between devices: 8.95 us -> 12.6 us  [shards(): lax.ppermute(face[0], 'brick', near_pairs)]
    pallas_call x3 -> x4, Pallas kernels: 38.1 us -> 41.4 us  [apply_bands(): pl.pallas_call(call, grid=(count,), in_specs=in_specs, out_specs=[pl.Bloc...]
    ppermute x3 -> x4, starting transfers between devices: 4.71 us -> 5.95 us  [shards(): lax.ppermute(face[1], 'brick', far_pairs)]
  transfers between devices with their start and end apart: 9 -> 11, of which waited for: 5 -> 6; matrix products, arithmetic and copies ran while one was open for 0% -> 0% of each run, Pallas kernels for 37% -> 42%
where the time goes in v1:
time: 119 us
  Pallas kernels  63.5 us (53%)
  waiting for transfers between devices  33.3 us (28%)
  starting transfers between devices  20.1 us (17%)
  local copies, waits for them, and re-layouts  1.63 us (1%)
    pallas_call x4, Pallas kernels, apply_bands(): pl.pallas_call(call, grid=(count,), in_specs=in_specs, out_specs=[pl.Bloc...  41.4 us
    ppermute x4, waiting for transfers between devices, shards(): lax.ppermute(face[0], 'brick', near_pairs)  14.7 us
    ppermute x1, waiting for transfers between devices, swaps(): lax.ppermute(turning, 'ka', [(i, (i + 2) % size) for i in range(size)])  14.2 us
    ppermute x4, starting transfers between devices, shards(): lax.ppermute(face[0], 'brick', near_pairs)  12.6 us
    pallas_call x1, Pallas kernels, front(): pl.pallas_call(functools.partial(front_body, planes, 1.0 / (2.0 * total),...  11.4 us
    ppermute x4, starting transfers between devices, shards(): lax.ppermute(face[1], 'brick', far_pairs)  5.95 us
    pallas_call x1, Pallas kernels, potential_of(): pl.pallas_call(functools.partial(potential_body, rows), in_specs=[whole]...  4.33 us
    pallas_call x2, Pallas kernels, add(): pl.pallas_call(add_body, in_specs=[whole, whole], out_specs=whole, out_sh...  3.41 us
  transfers between devices with their start and end apart: 11, of which 6 were waited for; matrix products, arithmetic and copies ran while one was open for 0% of the time, Pallas kernels for 42%

profile of v1, /device:TPU:0, one launch (start us, length us, event | category | flops | bytes accessed | tf_op | source)
XLA Modules:
  0.0 118.6 jit_solution(12685467231470906986)
XLA Ops:
  0.0 3.0 %edges.1 = (bf16[2,4,288,128]{3,2,1,0:T(8,128)(2,1)}, bf16[2,4,288,128]{3,2,1,0:T(8,128)(2,1)}) custom-call(bf16[8,4,1152,128]{3,2,1,0:T(8,128)(2,1)} %bitcast.24), custom_call_target="tpu_custom_call" | custom-call | tf_op jit(solution)/shard_map/edges/pallas_call | solution.py:104
  3.0 3.0 %collective-permute-start.3 = (bf16[2,4,288,128]{3,2,1,0:T(8,128)(2,1)}, bf16[2,4,288,128]{3,2,1,0:T(8,128)(2,1)}, u32[]{:S(2)}, u32[]{:S(2)}) collective-permute-start(bf16[2,4,288,128]{3,2,1,0:T(8,128)(2,1)} %get-tuple-element.48.refs_0_), channel_id=1, source_target_pairs={{0,1},{1,0},{2,3},{3,2},{4,5},{5,4},{6,7},{7,6},{8,9},{9,8},{10,11... | collective-permute-start | bytes 1769480 | tf_op jit(solution)/shard_map/ppermute | solution.py:451
  6.0 1.5 %collective-permute-start.4 = (bf16[2,4,288,128]{3,2,1,0:T(8,128)(2,1)}, bf16[2,4,288,128]{3,2,1,0:T(8,128)(2,1)}, u32[]{:S(2)}, u32[]{:S(2)}) collective-permute-start(bf16[2,4,288,128]{3,2,1,0:T(8,128)(2,1)} %get-tuple-element.49.refs_1_), channel_id=1, source_target_pairs={{1,2},{2,1},{3,4},{4,3},{5,6},{6,5},{9,10},{10,9},{11,12},{12,11},... | collective-permute-start | bytes 1769480 | tf_op jit(solution)/shard_map/ppermute | solution.py:451
  7.5 11.4 %front.1 = (bf16[2,8,144,128]{3,2,1,0:T(8,128)(2,1)S(1)}, bf16[2,8,144,128]{3,2,1,0:T(8,128)(2,1)}, bf16[2,4,288,128]{3,2,1,0:T(8,128)(2,1)}, bf16[2,4,288,128]{...) custom-call(s32[8]{0:T(128)} %mult_ref.1, ...), custom_call_target="tpu_custom_call" | custom-call | tf_op jit(solution)/shard_map/front/pallas_call | solution.py:176
  18.9 3.5 %collective-permute-start.5 = (bf16[2,4,288,128]{3,2,1,0:T(8,128)(2,1)}, bf16[2,4,288,128]{3,2,1,0:T(8,128)(2,1)}, u32[]{:S(2)}, u32[]{:S(2)}) collective-permute-start(bf16[2,4,288,128]{3,2,1,0:T(8,128)(2,1)} %get-tuple-element.60), channel_id=1, source_target_pairs={{0,1},{1,0},{2,3},{3,2},{4,5},{5,4},{6,7},{7,6},{8,9},{9,8},{10,11... | collective-permute-start | bytes 1769480 | tf_op jit(solution)/shard_map/ppermute | solution.py:451
  22.4 1.5 %collective-permute-start.6 = (bf16[2,4,288,128]{3,2,1,0:T(8,128)(2,1)}, bf16[2,4,288,128]{3,2,1,0:T(8,128)(2,1)}, u32[]{:S(2)}, u32[]{:S(2)}) collective-permute-start(bf16[2,4,288,128]{3,2,1,0:T(8,128)(2,1)} %get-tuple-element.61), channel_id=1, source_target_pairs={{1,2},{2,1},{3,4},{4,3},{5,6},{6,5},{9,10},{10,9},{11,12},{12,11},... | collective-permute-start | bytes 1769480 | tf_op jit(solution)/shard_map/ppermute | solution.py:451
  23.9 24.3 %while.12 = (s32[]{:T(128)}, bf16[2,1152,128]{2,1,0:T(8,128)(2,1)S(1)}, bf16[2,1152,128]{2,1,0:T(8,128)(2,1)}, s32[]{:T(128)}, s32[]{:T(128)}) while((s32[]{:T(128)}, bf16[2,1152,128]{2,1,0:T(8,128)(2,1)S(1)}, bf16[2,1152,128]{2,1,0:T(8,128)(2,1)}, s32[]{:T(128)}, s32[]{:T(128)}) %tuple.22), condition=%wide.region_1.0_spmd, body=%wide.region_0.0_spmd.sunk | while | flops 2 | bytes 9437393 | solution.py:237
  23.9 2.3 %collective-permute-done.b_ref = bf16[2,1152,128]{2,1,0:T(8,128)(2,1)} collective-permute-done((bf16[2,1152,128]{2,1,0:T(8,128)(2,1)}, bf16[2,1152,128]{2,1,0:T(8,128)(2,1)}, u32[]{:S(2)}, u32[]{:S(2)}) %collective-permute-start) | collective-permute-done | bytes 589856 | tf_op jit(solution)/shard_map/while/body/ppermute | solution.py:229
  26.2 2.0 %add.11.a_ref = bf16[2,1152,128]{2,1,0:T(8,128)(2,1)} custom-call(bf16[2,1152,128]{2,1,0:T(8,128)(2,1)S(1)} %get-tuple-element.109.a_ref, bf16[2,1152,128]{2,1,0:T(8,128)(2,1)} %collective-permute-done.b_ref), custom_call_target="tpu_custom_call" | custom-call | tf_op jit(solution)/shard_map/while/body/add/pallas_call | solution.py:207
  28.3 1.5 %collective-permute-start.1 = (bf16[2,1152,128]{2,1,0:T(8,128)(2,1)}, bf16[2,1152,128]{2,1,0:T(8,128)(2,1)}, u32[]{:S(2)}, u32[]{:S(2)}) collective-permute-start(bf16[2,1152,128]{2,1,0:T(8,128)(2,1)} %add.11.a_ref), channel_id=1, source_target_pairs={{0,16},{8,24},{16,0},{24,8},{1,17},{9,25},{17,1},{25,9},{2,18},{10... | collective-permute-start | bytes 1769480 | tf_op jit(solution)/shard_map/while/body/ppermute | solution.py:232
  29.7 14.2 %collective-permute-done.1.b_ref = bf16[2,1152,128]{2,1,0:T(8,128)(2,1)} collective-permute-done((bf16[2,1152,128]{2,1,0:T(8,128)(2,1)}, bf16[2,1152,128]{2,1,0:T(8,128)(2,1)}, u32[]{:S(2)}, u32[]{:S(2)}) %collective-permute-start.1) | collective-permute-done | bytes 589856 | tf_op jit(solution)/shard_map/while/body/ppermute | solution.py:232
  43.9 1.4 %add.12 = bf16[2,1152,128]{2,1,0:T(8,128)(2,1)S(1)} custom-call(bf16[2,1152,128]{2,1,0:T(8,128)(2,1)} %add.11.a_ref, bf16[2,1152,128]{2,1,0:T(8,128)(2,1)} %collective-permute-done.1.b_ref), custom_call_target="tpu_custom_call" | custom-call | tf_op jit(solution)/shard_map/while/body/add/pallas_call | solution.py:207
  45.4 2.0 %collective-permute-done.2 = bf16[2,1152,128]{2,1,0:T(8,128)(2,1)S(1)} collective-permute-done((bf16[2,1152,128]{2,1,0:T(8,128)(2,1)S(1)}, bf16[2,1152,128]{2,1,0:T(8,128)(2,1)S(1)}, u32[]{:S(2)}, u32[]{:S(2)}) %collective-permute-start.2) | collective-permute-done | bytes 589856 | tf_op jit(solution)/shard_map/while/body/ppermute | solution.py:234
  48.2 3.6 %collective-permute-start.9 = (bf16[2,4,288,128]{3,2,1,0:T(8,128)(2,1)}, bf16[2,4,288,128]{3,2,1,0:T(8,128)(2,1)}, u32[]{:S(2)}, u32[]{:S(2)}) collective-permute-start(bf16[2,4,288,128]{3,2,1,0:T(8,128)(2,1)} %get-tuple-element.56.refs_0_), channel_id=1, source_target_pairs={{0,1},{1,0},{2,3},{3,2},{4,5},{5,4},{6,7},{7,6},{8,9},{9,8},{10,11... | collective-permute-start | bytes 1769480 | tf_op jit(solution)/shard_map/ppermute | solution.py:451
  51.8 1.5 %collective-permute-start.10 = (bf16[2,4,288,128]{3,2,1,0:T(8,128)(2,1)}, bf16[2,4,288,128]{3,2,1,0:T(8,128)(2,1)}, u32[]{:S(2)}, u32[]{:S(2)}) collective-permute-start(bf16[2,4,288,128]{3,2,1,0:T(8,128)(2,1)} %get-tuple-element.57.refs_1_), channel_id=1, source_target_pairs={{1,2},{2,1},{3,4},{4,3},{5,6},{6,5},{9,10},{10,9},{11,12},{12,11},... | collective-permute-start | bytes 1769480 | tf_op jit(solution)/shard_map/ppermute | solution.py:451
  53.3 4.3 %potential.1.pot_ref = f32[4,144,8,128]{3,2,1,0:T(8,128)} custom-call(bf16[2,1152,128]{2,1,0:T(8,128)(2,1)S(1)} %get-tuple-element.52.refs_4_.mine_ref, bf16[2,1152,128]{2,1,0:T(8,128)(2,1)} %get-tuple-element.53.other_ref, f32[1152,128]{1,0:T(8,128)} %bitcast.31, f32[1152,128]{1,0:T(8,128)} %bitcast.32, bf16[2,4,288,128]{3,2,1,0:T(8,128)(2,1)} %get-tuple-element.56.refs_0_, ...), custom_call_target="tpu_custom_call" | custom-call | tf_op jit(solution)/shard_map/potential/pallas_call | solution.py:284
  57.6 10.3 %apply.4 = (bf16[8,4,1152,128]{3,2,1,0:T(8,128)(2,1)}, f32[8,128]{1,0:T(8,128)}) custom-call(bf16[8,4,1152,128]{3,2,1,0:T(8,128)(2,1)} %bitcast.26, f32[4,144,8,128]{3,2,1,0:T(8,128)} %potential.1.pot_ref, bf16[2,4,288,128]{3,2,1,0:T(8,128)(2,1)} %collective-permute-done.3.refs_2_.near_ref, bf16[2,4,288,128]{3,2,1,0:T(8,128)(2,1)} %collective-permute-done.4.refs_3_.far_ref), custom_call_target="tpu_custom_call" | custom-call | tf_op jit(solution)/shard_map/apply/pallas_call | solution.py:411
  68.0 2.6 %collective-permute-done.5.refs_2_.near_ref = bf16[2,4,288,128]{3,2,1,0:T(8,128)(2,1)} collective-permute-done((bf16[2,4,288,128]{3,2,1,0:T(8,128)(2,1)}, bf16[2,4,288,128]{3,2,1,0:T(8,128)(2,1)}, u32[]{:S(2)}, u32[]{:S(2)}) %collective-permute-start.5) | collective-permute-done | bytes 589856 | tf_op jit(solution)/shard_map/ppermute | solution.py:451
  70.6 2.5 %collective-permute-start.7 = (bf16[2,4,288,128]{3,2,1,0:T(8,128)(2,1)}, bf16[2,4,288,128]{3,2,1,0:T(8,128)(2,1)S(1)}, u32[]{:S(2)}, u32[]{:S(2)}) collective-permute-start(bf16[2,4,288,128]{3,2,1,0:T(8,128)(2,1)} %get-tuple-element.63), channel_id=1, source_target_pairs={{0,1},{1,0},{2,3},{3,2},{4,5},{5,4},{6,7},{7,6},{8,9},{9,8},{10,11... | collective-permute-start | bytes 1769480 | tf_op jit(solution)/shard_map/ppermute | solution.py:451
  73.1 1.5 %collective-permute-start.8 = (bf16[2,4,288,128]{3,2,1,0:T(8,128)(2,1)}, bf16[2,4,288,128]{3,2,1,0:T(8,128)(2,1)}, u32[]{:S(2)}, u32[]{:S(2)}) collective-permute-start(bf16[2,4,288,128]{3,2,1,0:T(8,128)(2,1)} %get-tuple-element.64), channel_id=1, source_target_pairs={{1,2},{2,1},{3,4},{4,3},{5,6},{6,5},{9,10},{10,9},{11,12},{12,11},... | collective-permute-start | bytes 1769480 | tf_op jit(solution)/shard_map/ppermute | solution.py:451
  74.6 10.3 %apply.5 = (bf16[8,4,1152,128]{3,2,1,0:T(8,128)(2,1)}, f32[8,128]{1,0:T(8,128)}) custom-call(bf16[8,4,1152,128]{3,2,1,0:T(8,128)(2,1)} %bitcast.27, f32[4,144,8,128]{3,2,1,0:T(8,128)} %potential.1.pot_ref, bf16[2,4,288,128]{3,2,1,0:T(8,128)(2,1)} %collective-permute-done.5.refs_2_.near_ref, ...), custom_call_target="tpu_custom_call", output_to_operand_aliasing={{0}: (4, {})} | custom-call | tf_op jit(solution)/shard_map/apply/pallas_call | solution.py:411
  84.9 11.0 %collective-permute-done.9.near_ref = bf16[2,4,288,128]{3,2,1,0:T(8,128)(2,1)} collective-permute-done((bf16[2,4,288,128]{3,2,1,0:T(8,128)(2,1)}, bf16[2,4,288,128]{3,2,1,0:T(8,128)(2,1)}, u32[]{:S(2)}, u32[]{:S(2)}) %collective-permute-start.9) | collective-permute-done | bytes 589856 | tf_op jit(solution)/shard_map/ppermute | solution.py:451
  95.9 10.3 %apply.6 = (bf16[8,4,1152,128]{3,2,1,0:T(8,128)(2,1)}, f32[8,128]{1,0:T(8,128)}) custom-call(bf16[8,4,1152,128]{3,2,1,0:T(8,128)(2,1)} %bitcast.28, f32[4,144,8,128]{3,2,1,0:T(8,128)} %potential.1.pot_ref, bf16[2,4,288,128]{3,2,1,0:T(8,128)(2,1)} %collective-permute-done.9.near_ref, ...), custom_call_target="tpu_custom_call", output_to_operand_aliasing={{0}: (4, {})} | custom-call | tf_op jit(solution)/shard_map/apply/pallas_call | solution.py:411
  108.2 10.3 %apply.7 = (bf16[8,4,1152,128]{3,2,1,0:T(8,128)(2,1)}, f32[8,128]{1,0:T(8,128)}) custom-call(bf16[8,4,1152,128]{3,2,1,0:T(8,128)(2,1)} %bitcast.29, f32[4,144,8,128]{3,2,1,0:T(8,128)} %potential.1.pot_ref, bf16[2,4,288,128]{3,2,1,0:T(8,128)(2,1)} %copy-done.1, ...), custom_call_target="tpu_custom_call", output_to_operand_aliasing={{0}: (4, {})} | custom-call | tf_op jit(solution)/shard_map/apply/pallas_call | solution.py:411
  (14 shorter events, 2.9 us)
Async XLA Ops:
  3.0 45.2 %collective-permute-start.3 = (bf16[2,4,288,128]{3,2,1,0:T(8,128)(2,1)}, bf16[2,4,288,128]{3,2,1,0:T(8,128)(2,1)}, u32[]{:S(2)}, u32[]{:S(2)}) collective-permute-start(bf16[2,4,288,128]{3,2,1,0:T(8,128)(2,1)} %get-tuple-element.48.refs_0_), channel_id=1, source_target_pairs={{0,1},{1,0},{2,3},{3,2},{4,5},{5,4},{6,7},{7,6},{8,9},{9,8},{10,11... | collective-permute-start | bytes 1769480 | tf_op jit(solution)/shard_map/ppermute | solution.py:451
  6.0 42.2 %collective-permute-start.4 = (bf16[2,4,288,128]{3,2,1,0:T(8,128)(2,1)}, bf16[2,4,288,128]{3,2,1,0:T(8,128)(2,1)}, u32[]{:S(2)}, u32[]{:S(2)}) collective-permute-start(bf16[2,4,288,128]{3,2,1,0:T(8,128)(2,1)} %get-tuple-element.49.refs_1_), channel_id=1, source_target_pairs={{1,2},{2,1},{3,4},{4,3},{5,6},{6,5},{9,10},{10,9},{11,12},{12,11},... | collective-permute-start | bytes 1769480 | tf_op jit(solution)/shard_map/ppermute | solution.py:451
  18.9 51.7 %collective-permute-start.5 = (bf16[2,4,288,128]{3,2,1,0:T(8,128)(2,1)}, bf16[2,4,288,128]{3,2,1,0:T(8,128)(2,1)}, u32[]{:S(2)}, u32[]{:S(2)}) collective-permute-start(bf16[2,4,288,128]{3,2,1,0:T(8,128)(2,1)} %get-tuple-element.60), channel_id=1, source_target_pairs={{0,1},{1,0},{2,3},{3,2},{4,5},{5,4},{6,7},{7,6},{8,9},{9,8},{10,11... | collective-permute-start | bytes 1769480 | tf_op jit(solution)/shard_map/ppermute | solution.py:451
  22.4 48.2 %collective-permute-start.6 = (bf16[2,4,288,128]{3,2,1,0:T(8,128)(2,1)}, bf16[2,4,288,128]{3,2,1,0:T(8,128)(2,1)}, u32[]{:S(2)}, u32[]{:S(2)}) collective-permute-start(bf16[2,4,288,128]{3,2,1,0:T(8,128)(2,1)} %get-tuple-element.61), channel_id=1, source_target_pairs={{1,2},{2,1},{3,4},{4,3},{5,6},{6,5},{9,10},{10,9},{11,12},{12,11},... | collective-permute-start | bytes 1769480 | tf_op jit(solution)/shard_map/ppermute | solution.py:451
  23.9 2.3 %collective-permute-start = (bf16[2,1152,128]{2,1,0:T(8,128)(2,1)}, bf16[2,1152,128]{2,1,0:T(8,128)(2,1)}, u32[]{:S(2)}, u32[]{:S(2)}) collective-permute-start(bf16[2,1152,128]{2,1,0:T(8,128)(2,1)} %get-tuple-element.110), channel_id=1, source_target_pairs={{0,8},{8,0},{16,24},{24,16},{1,9},{9,1},{17,25},{25,17},{2,10},{10... | collective-permute-start | bytes 1769480 | tf_op jit(solution)/shard_map/while/body/ppermute | solution.py:229
  28.3 15.7 %collective-permute-start.1 = (bf16[2,1152,128]{2,1,0:T(8,128)(2,1)}, bf16[2,1152,128]{2,1,0:T(8,128)(2,1)}, u32[]{:S(2)}, u32[]{:S(2)}) collective-permute-start(bf16[2,1152,128]{2,1,0:T(8,128)(2,1)} %add.11.a_ref), channel_id=1, source_target_pairs={{0,16},{8,24},{16,0},{24,8},{1,17},{9,25},{17,1},{25,9},{2,18},{10... | collective-permute-start | bytes 1769480 | tf_op jit(solution)/shard_map/while/body/ppermute | solution.py:232
  45.3 2.1 %collective-permute-start.2 = (bf16[2,1152,128]{2,1,0:T(8,128)(2,1)S(1)}, bf16[2,1152,128]{2,1,0:T(8,128)(2,1)S(1)}, u32[]{:S(2)}, u32[]{:S(2)}) collective-permute-start(bf16[2,1152,128]{2,1,0:T(8,128)(2,1)S(1)} %add.12), channel_id=1, source_target_pairs={{0,8},{8,0},{16,24},{24,16},{1,9},{9,1},{17,25},{25,17},{2,10},{10... | collective-permute-start | bytes 1769480 | tf_op jit(solution)/shard_map/while/body/ppermute | solution.py:234
  47.4 0.8 copy-start
  48.2 47.7 %collective-permute-start.9 = (bf16[2,4,288,128]{3,2,1,0:T(8,128)(2,1)}, bf16[2,4,288,128]{3,2,1,0:T(8,128)(2,1)}, u32[]{:S(2)}, u32[]{:S(2)}) collective-permute-start(bf16[2,4,288,128]{3,2,1,0:T(8,128)(2,1)} %get-tuple-element.56.refs_0_), channel_id=1, source_target_pairs={{0,1},{1,0},{2,3},{3,2},{4,5},{5,4},{6,7},{7,6},{8,9},{9,8},{10,11... | collective-permute-start | bytes 1769480 | tf_op jit(solution)/shard_map/ppermute | solution.py:451
  51.8 44.1 %collective-permute-start.10 = (bf16[2,4,288,128]{3,2,1,0:T(8,128)(2,1)}, bf16[2,4,288,128]{3,2,1,0:T(8,128)(2,1)}, u32[]{:S(2)}, u32[]{:S(2)}) collective-permute-start(bf16[2,4,288,128]{3,2,1,0:T(8,128)(2,1)} %get-tuple-element.57.refs_1_), channel_id=1, source_target_pairs={{1,2},{2,1},{3,4},{4,3},{5,6},{6,5},{9,10},{10,9},{11,12},{12,11},... | collective-permute-start | bytes 1769480 | tf_op jit(solution)/shard_map/ppermute | solution.py:451
  70.6 36.8 %collective-permute-start.7 = (bf16[2,4,288,128]{3,2,1,0:T(8,128)(2,1)}, bf16[2,4,288,128]{3,2,1,0:T(8,128)(2,1)S(1)}, u32[]{:S(2)}, u32[]{:S(2)}) collective-permute-start(bf16[2,4,288,128]{3,2,1,0:T(8,128)(2,1)} %get-tuple-element.63), channel_id=1, source_target_pairs={{0,1},{1,0},{2,3},{3,2},{4,5},{5,4},{6,7},{7,6},{8,9},{9,8},{10,11... | collective-permute-start | bytes 1769480 | tf_op jit(solution)/shard_map/ppermute | solution.py:451
  73.1 34.3 %collective-permute-start.8 = (bf16[2,4,288,128]{3,2,1,0:T(8,128)(2,1)}, bf16[2,4,288,128]{3,2,1,0:T(8,128)(2,1)}, u32[]{:S(2)}, u32[]{:S(2)}) collective-permute-start(bf16[2,4,288,128]{3,2,1,0:T(8,128)(2,1)} %get-tuple-element.64), channel_id=1, source_target_pairs={{1,2},{2,1},{3,4},{4,3},{5,6},{6,5},{9,10},{10,9},{11,12},{12,11},... | collective-permute-start | bytes 1769480 | tf_op jit(solution)/shard_map/ppermute | solution.py:451
  107.4 0.8 copy-start.1

commit v2 on v1

--- a/solution.py
+++ b/solution.py
@@ -16,6 +16,7 @@
 PACK = 16
 FLOOR_FRACTION = 0.05
 VMEM_LIMIT = 63 * 1024 * 1024
+UNROLL = 2
 SMALL = pl.CostEstimate(flops=0, bytes_accessed=0, transcendentals=0)
 
 
@@ -292,16 +293,11 @@
     )(mine, other, core, local, *after)
 
 
-def apply_body(planes, rows, x_ref, pot_ref, near_ref, far_ref, carry_ref, out_ref, token_ref, wide, ends, turned, flat):
-    segment = rows // SUB
+def hamiltonian(planes, x_ref, pot_ref, ends, flat, wide, turned):
+    segment = wide.shape[1]
     stride = planes * TRIPLE
     steps = segment // stride
-    near_slot = jnp.where(even_brick(), 1, 0)
-    spread, unspread = spread_matrix(False), spread_matrix(True)
-
-    for c in range(4):
-        ends[near_slot, c] = near_ref[0, c].astype(jnp.float32).reshape(ends.shape[2:])
-        ends[1 - near_slot, c] = far_ref[0, c].astype(jnp.float32).reshape(ends.shape[2:])
+    spread = spread_matrix(False)
 
     def load(i, unused):
         block = jnp.concatenate([gathered(lambda at: x_ref[0, c, at, :], segment, i) for c in range(4)], axis=1)
@@ -348,10 +344,16 @@
         )
         sums = []
         for tile in range(TRIPLE):
-            below = ends[0, c, j * TRIPLE + tile] if plane == 0 else wide[c, spot[tile] - 1]
-            above = ends[1, c, j * TRIPLE + tile] if plane == planes - 1 else wide[c, spot[tile] + 1]
-            along = pltpu.roll(plus[tile], LANES - 1, 1) + pltpu.roll(minus[tile], 1, 1)
-            sums.append((across[tile] + along) + (below + above))
+            total = across[tile] + (pltpu.roll(plus[tile], LANES - 1, 1) + pltpu.roll(minus[tile], 1, 1))
+            if plane > 0:
+                total = total + wide[c, spot[tile] - 1]
+            elif ends is not None:
+                total = total + ends[0, c, j * TRIPLE + tile]
+            if plane < planes - 1:
+                total = total + wide[c, spot[tile] + 1]
+            elif ends is not None:
+                total = total + ends[1, c, j * TRIPLE + tile]
+            sums.append(total)
         return (v0, v1, v2), sums
 
     def step(j, unused):
@@ -367,70 +369,145 @@
                 flat[3, spot] = bx * b + by * a + diag_down * f - 0.5 * ndi[tile]
         return unused
 
-    lax.fori_loop(0, steps, step, 0)
-
-    def store(i, unused):
-        at = pl.ds(i * PACK, PACK)
-        block = jnp.concatenate([flat[c, at].reshape(PACK * SUB, LANES) for c in range(4)], axis=1)
-        values = product(unspread, block.astype(jnp.bfloat16)).astype(jnp.bfloat16)
+    lax.fori_loop(0, steps, step, 0, unroll=UNROLL)
+
+
+def store_rows(parts, i, out_ref):
+    block = jnp.concatenate([part.astype(jnp.bfloat16) for part in parts], axis=1)
+    values = product(spread_matrix(True), block).astype(jnp.bfloat16)
+    for c in range(4):
+        for s in range(SUB):
+            out_ref[0, c, s, pl.ds(i * PACK, PACK), :] = values[s * PACK : (s + 1) * PACK, c * LANES : (c + 1) * LANES]
+
+
+def apply_body(planes, x_ref, pot_ref, near_ref, far_ref, *refs):
+    out_ref, token_ref, wide, turned, ends, flat = refs[-6:]
+    near_slot = jnp.where(even_brick(), 1, 0)
+    for c in range(4):
+        ends[near_slot, c] = near_ref[0, c].astype(jnp.float32).reshape(ends.shape[2:])
+        ends[1 - near_slot, c] = far_ref[0, c].astype(jnp.float32).reshape(ends.shape[2:])
+    hamiltonian(planes, x_ref, pot_ref, ends, flat, wide, turned)
+    for i in range(wide.shape[1] // PACK):
+        store_rows([flat[c, pl.ds(i * PACK, PACK)].reshape(PACK * SUB, LANES) for c in range(4)], i, out_ref)
+
+
+def ahead_body(planes, x_ref, pot_ref, *refs):
+    flat_ref, token_ref, wide, turned = refs[-4:]
+    hamiltonian(planes, x_ref, pot_ref, None, flat_ref.at[0], wide, turned)
+
+
+def finish_body(planes, flat_ref, near_ref, far_ref, *refs):
+    out_ref, token_ref = refs[-2:]
+    even = even_brick()
+    per = PACK // planes
+    for i in range(flat_ref.shape[2] // PACK):
+        outside = pl.ds(i * per * SUB, per * SUB)
+        parts = []
         for c in range(4):
-            for s in range(SUB):
-                out_ref[0, c, pl.ds(pl.multiple_of(s * segment + i * PACK, PACK), PACK), :] = values[
-                    s * PACK : (s + 1) * PACK, c * LANES : (c + 1) * LANES
-                ]
-        return unused
-
-    lax.fori_loop(0, segment // PACK, store, 0, unroll=True)
-
-
-def apply_bands(x, potential, near, far, planes, start, carry):
-    count, rows = near.shape[0], x.shape[2]
+            near = near_ref[0, c, outside, :].astype(jnp.float32).reshape(per, SUB, LANES)
+            far = far_ref[0, c, outside, :].astype(jnp.float32).reshape(per, SUB, LANES)
+            below, above = jnp.where(even, far, near), jnp.where(even, near, far)
+            pieces = []
+            for q in range(PACK):
+                piece = flat_ref[0, c, i * PACK + q]
+                if q % planes == 0:
+                    piece = piece - 0.5 * below[q // planes]
+                if q % planes == planes - 1:
+                    piece = piece - 0.5 * above[q // planes]
+                pieces.append(piece)
+            parts.append(jnp.concatenate(pieces, axis=0))
+        store_rows(parts, i, out_ref)
+
+
+def per_band(body, name, grid, inputs, in_specs, output, out_spec, carry, after, scratch):
+    anywhere = pl.BlockSpec(memory_space=pl.ANY)
+    carried = () if carry is None else (carry,)
+    return pl.pallas_call(
+        body,
+        grid=grid,
+        in_specs=in_specs + [anywhere] * (len(carried) + len(after)),
+        out_specs=[out_spec, anywhere],
+        out_shape=[
+            jax.ShapeDtypeStruct(*output),
+            jax.ShapeDtypeStruct((SUB, LANES), jnp.float32),
+        ],
+        input_output_aliases={len(inputs): 0} if carried else {},
+        scratch_shapes=scratch,
+        compiler_params=pltpu.CompilerParams(vmem_limit_bytes=VMEM_LIMIT),
+        cost_estimate=SMALL,
+        name=name,
+    )(*inputs, *carried, *after)
+
+
+def stencil_specs(rows, planes, start):
     segment = rows // SUB
-    stride = planes * TRIPLE
-    tiles = rows // planes
-    halo = pl.BlockSpec((1, 4, tiles, LANES), lambda b: (b, 0, 0, 0))
-    body = functools.partial(apply_body, planes, rows)
+    scratch = [
+        pltpu.VMEM((4, segment, SUB, LANES), jnp.float32),
+        pltpu.VMEM((4, segment + 2 * planes * TRIPLE, SUB, LANES), jnp.float32),
+    ]
     in_specs = [
         pl.BlockSpec((1, 4, rows, LANES), lambda b: (start + b, 0, 0, 0)),
         pl.BlockSpec((4, segment, SUB, LANES), lambda b: (0, 0, 0, 0)),
-        halo,
-        halo,
     ]
-    operands = [x, potential, near, far]
-    aliases = {}
-    if carry is not None:
-        in_specs.append(pl.BlockSpec(memory_space=pl.ANY))
-        operands.append(carry)
-        aliases = {4: 0}
-        call = body
-    else:
-
-        def call(x_ref, pot_ref, near_ref, far_ref, *rest):
-            body(x_ref, pot_ref, near_ref, far_ref, None, *rest)
-
-    return pl.pallas_call(
-        call,
-        grid=(count,),
-        in_specs=in_specs,
-        out_specs=[
-            pl.BlockSpec((1, 4, rows, LANES), lambda b: (start + b, 0, 0, 0)),
-            pl.BlockSpec(memory_space=pl.ANY),
-        ],
-        out_shape=[
-            jax.ShapeDtypeStruct(x.shape, jnp.bfloat16),
-            jax.ShapeDtypeStruct((SUB, LANES), jnp.float32),
-        ],
-        input_output_aliases=aliases,
-        scratch_shapes=[
-            pltpu.VMEM((4, segment, SUB, LANES), jnp.float32),
-            pltpu.VMEM((2, 4, tiles // SUB, SUB, LANES), jnp.float32),
-            pltpu.VMEM((4, segment + 2 * stride, SUB, LANES), jnp.float32),
-            pltpu.VMEM((4, segment, SUB, LANES), jnp.float32),
-        ],
-        compiler_params=pltpu.CompilerParams(vmem_limit_bytes=VMEM_LIMIT),
-        cost_estimate=SMALL,
-        name="apply",
-    )(*operands)
+    return in_specs, scratch
+
+
+def apply_bands(x, potential, near, far, planes, start, carry, after):
+    count, bands, rows = near.shape[0], x.shape[0], x.shape[2]
+    segment, tiles = rows // SUB, rows // planes
+    in_specs, scratch = stencil_specs(rows, planes, start)
+    halo = pl.BlockSpec((1, 4, tiles, LANES), lambda b: (b, 0, 0, 0))
+    scratch += [
+        pltpu.VMEM((2, 4, tiles // SUB, SUB, LANES), jnp.float32),
+        pltpu.VMEM((4, segment, SUB, LANES), jnp.float32),
+    ]
+    return per_band(
+        functools.partial(apply_body, planes),
+        "apply",
+        (count,),
+        (x, potential, near, far),
+        in_specs + [halo, halo],
+        ((bands, 4, SUB, segment, LANES), jnp.bfloat16),
+        pl.BlockSpec((1, 4, SUB, segment, LANES), lambda b: (start + b, 0, 0, 0, 0)),
+        carry,
+        after,
+        scratch,
+    )
+
+
+def ahead_of(x, potential, planes, start, count, after):
+    segment = x.shape[2] // SUB
+    in_specs, scratch = stencil_specs(x.shape[2], planes, start)
+    return per_band(
+        functools.partial(ahead_body, planes),
+        "ahead",
+        (count,),
+        (x, potential),
+        in_specs,
+        ((count, 4, segment, SUB, LANES), jnp.float32),
+        pl.BlockSpec((1, 4, segment, SUB, LANES), lambda b: (b, 0, 0, 0, 0)),
+        None,
+        after,
+        scratch,
+    )
+
+
+def finish(flat, near, far, planes, start, carry):
+    count, segment = flat.shape[0], flat.shape[2]
+    part = segment // 3 if segment % (3 * PACK) == 0 else segment
+    halo = pl.BlockSpec((1, 4, part // planes * SUB, LANES), lambda b, i: (b, 0, i, 0))
+    return per_band(
+        functools.partial(finish_body, planes),
+        "finish",
+        (count, segment // part),
+        (flat, near, far),
+        [pl.BlockSpec((1, 4, part, SUB, LANES), lambda b, i: (b, 0, i, 0, 0)), halo, halo],
+        (carry.shape, carry.dtype),
+        pl.BlockSpec((1, 4, SUB, part, LANES), lambda b, i: (start + b, 0, 0, i, 0)),
+        carry,
+        (),
+        [],
+    )
 
 
 def chunk_sizes(bands):
@@ -460,13 +537,20 @@
         gated = gate(*faces[2], halos[0] + (density[0],))
         halos.append(swap(gated))
     potential = potential_of(*density, core, local, gated)
-    out, token = None, ()
+    last = len(starts) - 1
+    out, token, flat = None, (), None
     for k, start in enumerate(starts):
-        if 0 < k < len(starts) - 2:
+        if 0 < k < last - 1:
             halos.append(swap(gate(*faces[k + 2], halos[k] + token)))
-        out, done = apply_bands(x, potential, *halos[k], planes, start, out)
+        if k > 0 and k == last - 1:
+            flat, done = ahead_of(x, potential, planes, starts[last], sizes[last], token)
+            token = (done,)
+        if flat is None or k < last:
+            out, done = apply_bands(x, potential, *halos[k], planes, start, out, token)
+        else:
+            out, done = finish(flat, *halos[k], planes, start, out)
         token = (done,)
-    return planes_view(out, planes)
+    return planes_view(out.reshape(x.shape), planes)
 
 
 def solution(mesh):

time: 119 us -> 115 us (0.966)
  waiting for transfers between devices: 33.3 us -> 27 us
  Pallas kernels: 63.5 us -> 65.6 us
    ppermute x4, waiting for transfers between devices: 14.7 us -> 8.42 us  [shards(): lax.ppermute(face[0], 'brick', near_pairs)]
    pallas_call x4 -> x5, Pallas kernels: 41.4 us -> 43.5 us  [per_band(): pl.pallas_call(body, grid=grid, in_specs=in_specs + [anywhere] * (len(car...]
  transfers between devices with their start and end apart: 11 -> 11, of which waited for: 6 -> 6; matrix products, arithmetic and copies ran while one was open for 0% -> 0% of each run, Pallas kernels for 42% -> 49%
where the time goes in v2:
time: 115 us; the launch traced here: 114 us
  Pallas kernels  65.6 us (57%)
  waiting for transfers between devices  27 us (23%)
  starting transfers between devices  20.2 us (18%)
  local copies, waits for them, and re-layouts  1.68 us (1%)
    pallas_call x5, Pallas kernels, per_band(): pl.pallas_call(body, grid=grid, in_specs=in_specs + [anywhere] * (len(car...  43.5 us
    ppermute x1, waiting for transfers between devices, swaps(): lax.ppermute(turning, 'ka', [(i, (i + 2) % size) for i in range(size)])  14.2 us
    ppermute x4, starting transfers between devices, shards(): lax.ppermute(face[0], 'brick', near_pairs)  12.6 us
    pallas_call x1, Pallas kernels, front(): pl.pallas_call(functools.partial(front_body, planes, 1.0 / (2.0 * total),...  11.4 us
    ppermute x4, waiting for transfers between devices, shards(): lax.ppermute(face[0], 'brick', near_pairs)  8.42 us
    ppermute x4, starting transfers between devices, shards(): lax.ppermute(face[1], 'brick', far_pairs)  5.97 us
    pallas_call x1, Pallas kernels, potential_of(): pl.pallas_call(functools.partial(potential_body, rows), in_specs=[whole]...  4.34 us
    pallas_call x2, Pallas kernels, add(): pl.pallas_call(add_body, in_specs=[whole, whole], out_specs=whole, out_sh...  3.4 us
  transfers between devices with their start and end apart: 11, of which 6 were waited for; matrix products, arithmetic and copies ran while one was open for 0% of the time, Pallas kernels for 49%

profile of v2, /device:TPU:0, one launch (start us, length us, event | category | flops | bytes accessed | tf_op | source)
XLA Modules:
  0.0 114.4 jit_solution(12562390876193436765)
XLA Ops:
  0.0 3.0 %edges.1 = (bf16[2,4,288,128]{3,2,1,0:T(8,128)(2,1)}, bf16[2,4,288,128]{3,2,1,0:T(8,128)(2,1)}) custom-call(bf16[8,4,1152,128]{3,2,1,0:T(8,128)(2,1)} %bitcast.24), custom_call_target="tpu_custom_call" | custom-call | tf_op jit(solution)/shard_map/edges/pallas_call | solution.py:105
  3.0 3.0 %collective-permute-start.3 = (bf16[2,4,288,128]{3,2,1,0:T(8,128)(2,1)}, bf16[2,4,288,128]{3,2,1,0:T(8,128)(2,1)}, u32[]{:S(2)}, u32[]{:S(2)}) collective-permute-start(bf16[2,4,288,128]{3,2,1,0:T(8,128)(2,1)} %get-tuple-element.51.refs_0_), channel_id=1, source_target_pairs={{0,1},{1,0},{2,3},{3,2},{4,5},{5,4},{6,7},{7,6},{8,9},{9,8},{10,11... | collective-permute-start | bytes 1769480 | tf_op jit(solution)/shard_map/ppermute | solution.py:528
  7.5 11.4 %front.1 = (bf16[2,8,144,128]{3,2,1,0:T(8,128)(2,1)S(1)}, bf16[2,8,144,128]{3,2,1,0:T(8,128)(2,1)}, bf16[2,4,288,128]{3,2,1,0:T(8,128)(2,1)}, bf16[2,4,288,128]{...) custom-call(s32[8]{0:T(128)} %mult_ref.1, ...), custom_call_target="tpu_custom_call" | custom-call | tf_op jit(solution)/shard_map/front/pallas_call | solution.py:177
  18.9 3.5 %collective-permute-start.5 = (bf16[2,4,288,128]{3,2,1,0:T(8,128)(2,1)}, bf16[2,4,288,128]{3,2,1,0:T(8,128)(2,1)}, u32[]{:S(2)}, u32[]{:S(2)}) collective-permute-start(bf16[2,4,288,128]{3,2,1,0:T(8,128)(2,1)} %get-tuple-element.61), channel_id=1, source_target_pairs={{0,1},{1,0},{2,3},{3,2},{4,5},{5,4},{6,7},{7,6},{8,9},{9,8},{10,11... | collective-permute-start | bytes 1769480 | tf_op jit(solution)/shard_map/ppermute | solution.py:528
  22.4 1.5 %collective-permute-start.6 = (bf16[2,4,288,128]{3,2,1,0:T(8,128)(2,1)}, bf16[2,4,288,128]{3,2,1,0:T(8,128)(2,1)}, u32[]{:S(2)}, u32[]{:S(2)}) collective-permute-start(bf16[2,4,288,128]{3,2,1,0:T(8,128)(2,1)} %get-tuple-element.62), channel_id=1, source_target_pairs={{1,2},{2,1},{3,4},{4,3},{5,6},{6,5},{9,10},{10,9},{11,12},{12,11},... | collective-permute-start | bytes 1769480 | tf_op jit(solution)/shard_map/ppermute | solution.py:528
  23.9 24.3 %while.12 = (s32[]{:T(128)}, bf16[2,1152,128]{2,1,0:T(8,128)(2,1)S(1)}, bf16[2,1152,128]{2,1,0:T(8,128)(2,1)}, s32[]{:T(128)}, s32[]{:T(128)}) while((s32[]{:T(128)}, bf16[2,1152,128]{2,1,0:T(8,128)(2,1)S(1)}, bf16[2,1152,128]{2,1,0:T(8,128)(2,1)}, s32[]{:T(128)}, s32[]{:T(128)}) %tuple.22), condition=%wide.region_1.0_spmd, body=%wide.region_0.0_spmd.sunk | while | flops 2 | bytes 9437393 | solution.py:238
  23.9 2.3 %collective-permute-done.b_ref = bf16[2,1152,128]{2,1,0:T(8,128)(2,1)} collective-permute-done((bf16[2,1152,128]{2,1,0:T(8,128)(2,1)}, bf16[2,1152,128]{2,1,0:T(8,128)(2,1)}, u32[]{:S(2)}, u32[]{:S(2)}) %collective-permute-start) | collective-permute-done | bytes 589856 | tf_op jit(solution)/shard_map/while/body/ppermute | solution.py:230
  26.2 2.0 %add.11.a_ref = bf16[2,1152,128]{2,1,0:T(8,128)(2,1)} custom-call(bf16[2,1152,128]{2,1,0:T(8,128)(2,1)S(1)} %get-tuple-element.115.a_ref, bf16[2,1152,128]{2,1,0:T(8,128)(2,1)} %collective-permute-done.b_ref), custom_call_target="tpu_custom_call" | custom-call | tf_op jit(solution)/shard_map/while/body/add/pallas_call | solution.py:208
  28.3 1.5 %collective-permute-start.1 = (bf16[2,1152,128]{2,1,0:T(8,128)(2,1)}, bf16[2,1152,128]{2,1,0:T(8,128)(2,1)}, u32[]{:S(2)}, u32[]{:S(2)}) collective-permute-start(bf16[2,1152,128]{2,1,0:T(8,128)(2,1)} %add.11.a_ref), channel_id=1, source_target_pairs={{0,16},{8,24},{16,0},{24,8},{1,17},{9,25},{17,1},{25,9},{2,18},{10... | collective-permute-start | bytes 1769480 | tf_op jit(solution)/shard_map/while/body/ppermute | solution.py:233
  29.7 14.2 %collective-permute-done.1.b_ref = bf16[2,1152,128]{2,1,0:T(8,128)(2,1)} collective-permute-done((bf16[2,1152,128]{2,1,0:T(8,128)(2,1)}, bf16[2,1152,128]{2,1,0:T(8,128)(2,1)}, u32[]{:S(2)}, u32[]{:S(2)}) %collective-permute-start.1) | collective-permute-done | bytes 589856 | tf_op jit(solution)/shard_map/while/body/ppermute | solution.py:233
  45.4 2.0 %collective-permute-done.2 = bf16[2,1152,128]{2,1,0:T(8,128)(2,1)S(1)} collective-permute-done((bf16[2,1152,128]{2,1,0:T(8,128)(2,1)S(1)}, bf16[2,1152,128]{2,1,0:T(8,128)(2,1)S(1)}, u32[]{:S(2)}, u32[]{:S(2)}) %collective-permute-start.2) | collective-permute-done | bytes 589856 | tf_op jit(solution)/shard_map/while/body/ppermute | solution.py:235
  48.2 3.6 %collective-permute-start.9 = (bf16[2,4,288,128]{3,2,1,0:T(8,128)(2,1)}, bf16[2,4,288,128]{3,2,1,0:T(8,128)(2,1)}, u32[]{:S(2)}, u32[]{:S(2)}) collective-permute-start(bf16[2,4,288,128]{3,2,1,0:T(8,128)(2,1)} %get-tuple-element.59.refs_0_), channel_id=1, source_target_pairs={{0,1},{1,0},{2,3},{3,2},{4,5},{5,4},{6,7},{7,6},{8,9},{9,8},{10,11... | collective-permute-start | bytes 1769480 | tf_op jit(solution)/shard_map/ppermute | solution.py:528
  51.8 1.5 %collective-permute-start.10 = (bf16[2,4,288,128]{3,2,1,0:T(8,128)(2,1)}, bf16[2,4,288,128]{3,2,1,0:T(8,128)(2,1)}, u32[]{:S(2)}, u32[]{:S(2)}) collective-permute-start(bf16[2,4,288,128]{3,2,1,0:T(8,128)(2,1)} %get-tuple-element.60.refs_1_), channel_id=1, source_target_pairs={{1,2},{2,1},{3,4},{4,3},{5,6},{6,5},{9,10},{10,9},{11,12},{12,11},... | collective-permute-start | bytes 1769480 | tf_op jit(solution)/shard_map/ppermute | solution.py:528
  53.3 4.3 %potential.1.pot_ref = f32[4,144,8,128]{3,2,1,0:T(8,128)} custom-call(bf16[2,1152,128]{2,1,0:T(8,128)(2,1)S(1)} %get-tuple-element.55.refs_4_.mine_ref, bf16[2,1152,128]{2,1,0:T(8,128)(2,1)} %get-tuple-element.56.other_ref, f32[1152,128]{1,0:T(8,128)} %bitcast.31, f32[1152,128]{1,0:T(8,128)} %bitcast.32, bf16[2,4,288,128]{3,2,1,0:T(8,128)(2,1)} %get-tuple-element.59.refs_0_, ...), custom_call_target="tpu_custom_call" | custom-call | tf_op jit(solution)/shard_map/potential/pallas_call | solution.py:285
  57.7 9.6 %apply.3 = (bf16[8,4,8,144,128]{4,3,2,1,0:T(8,128)(2,1)}, f32[8,128]{1,0:T(8,128)}) custom-call(bf16[8,4,1152,128]{3,2,1,0:T(8,128)(2,1)} %bitcast.26, f32[4,144,8,128]{3,2,1,0:T(8,128)} %potential.1.pot_ref, bf16[2,4,288,128]{3,2,1,0:T(8,128)(2,1)} %collective-permute-done.3.refs_2_.near_ref, bf16[2,4,288,128]{3,2,1,0:T(8,128)(2,1)} %collective-permute-done.4.refs_3_.far_ref), custom_call_target="tpu_custom_call" | custom-call | tf_op jit(solution)/shard_map/apply/pallas_call | solution.py:425
  67.3 3.3 %collective-permute-done.5.near_ref.refs_2_ = bf16[2,4,288,128]{3,2,1,0:T(8,128)(2,1)} collective-permute-done((bf16[2,4,288,128]{3,2,1,0:T(8,128)(2,1)}, bf16[2,4,288,128]{3,2,1,0:T(8,128)(2,1)}, u32[]{:S(2)}, u32[]{:S(2)}) %collective-permute-start.5) | collective-permute-done | bytes 589856 | tf_op jit(solution)/shard_map/ppermute | solution.py:528
  70.6 2.5 %collective-permute-start.7 = (bf16[2,4,288,128]{3,2,1,0:T(8,128)(2,1)}, bf16[2,4,288,128]{3,2,1,0:T(8,128)(2,1)S(1)}, u32[]{:S(2)}, u32[]{:S(2)}) collective-permute-start(bf16[2,4,288,128]{3,2,1,0:T(8,128)(2,1)} %get-tuple-element.69), channel_id=1, source_target_pairs={{0,1},{1,0},{2,3},{3,2},{4,5},{5,4},{6,7},{7,6},{8,9},{9,8},{10,11... | collective-permute-start | bytes 1769480 | tf_op jit(solution)/shard_map/ppermute | solution.py:528
  73.1 1.5 %collective-permute-start.8 = (bf16[2,4,288,128]{3,2,1,0:T(8,128)(2,1)}, bf16[2,4,288,128]{3,2,1,0:T(8,128)(2,1)}, u32[]{:S(2)}, u32[]{:S(2)}) collective-permute-start(bf16[2,4,288,128]{3,2,1,0:T(8,128)(2,1)} %get-tuple-element.70), channel_id=1, source_target_pairs={{1,2},{2,1},{3,4},{4,3},{5,6},{6,5},{9,10},{10,9},{11,12},{12,11},... | collective-permute-start | bytes 1769480 | tf_op jit(solution)/shard_map/ppermute | solution.py:528
  74.6 9.6 %apply.4 = (bf16[8,4,8,144,128]{4,3,2,1,0:T(8,128)(2,1)}, f32[8,128]{1,0:T(8,128)}) custom-call(bf16[8,4,1152,128]{3,2,1,0:T(8,128)(2,1)} %bitcast.27, f32[4,144,8,128]{3,2,1,0:T(8,128)} %potential.1.pot_ref, bf16[2,4,288,128]{3,2,1,0:T(8,128)(2,1)} %collective-permute-done.5.near_ref.refs_2_, ...), custom_call_target="tpu_custom_call", output_to_operand_aliasing={{0}: (4, {})} | custom-call | tf_op jit(solution)/shard_map/apply/pallas_call | solution.py:425
  84.2 8.5 %ahead.1 = (f32[2,4,144,8,128]{4,3,2,1,0:T(8,128)}, f32[8,128]{1,0:T(8,128)}) custom-call(bf16[8,4,1152,128]{3,2,1,0:T(8,128)(2,1)} %bitcast.28, f32[4,144,8,128]{3,2,1,0:T(8,128)} %potential.1.pot_ref, f32[8,128]{1,0:T(8,128)} %get-tuple-element.65.refs_0_), custom_call_target="tpu_custom_call" | custom-call | tf_op jit(solution)/shard_map/ahead/pallas_call | solution.py:425
  92.7 3.2 %collective-permute-done.9.near_ref = bf16[2,4,288,128]{3,2,1,0:T(8,128)(2,1)} collective-permute-done((bf16[2,4,288,128]{3,2,1,0:T(8,128)(2,1)}, bf16[2,4,288,128]{3,2,1,0:T(8,128)(2,1)}, u32[]{:S(2)}, u32[]{:S(2)}) %collective-permute-start.9) | collective-permute-done | bytes 589856 | tf_op jit(solution)/shard_map/ppermute | solution.py:528
  95.9 9.6 %apply.5 = (bf16[8,4,8,144,128]{4,3,2,1,0:T(8,128)(2,1)}, f32[8,128]{1,0:T(8,128)}) custom-call(bf16[8,4,1152,128]{3,2,1,0:T(8,128)(2,1)} %bitcast.29, f32[4,144,8,128]{3,2,1,0:T(8,128)} %potential.1.pot_ref, bf16[2,4,288,128]{3,2,1,0:T(8,128)(2,1)} %collective-permute-done.9.near_ref, ...), custom_call_target="tpu_custom_call", output_to_operand_aliasing={{0}: (4, {})} | custom-call | tf_op jit(solution)/shard_map/apply/pallas_call | solution.py:425
  105.5 1.9 %collective-permute-done.7.near_ref = bf16[2,4,288,128]{3,2,1,0:T(8,128)(2,1)S(1)} collective-permute-done((bf16[2,4,288,128]{3,2,1,0:T(8,128)(2,1)}, bf16[2,4,288,128]{3,2,1,0:T(8,128)(2,1)S(1)}, u32[]{:S(2)}, u32[]{:S(2)}) %collective-permute-start.7) | collective-permute-done | bytes 589856 | tf_op jit(solution)/shard_map/ppermute | solution.py:528
  108.2 6.2 %finish.1 = (bf16[8,4,8,144,128]{4,3,2,1,0:T(8,128)(2,1)}, f32[8,128]{1,0:T(8,128)}) custom-call(f32[2,4,144,8,128]{4,3,2,1,0:T(8,128)} %get-tuple-element.66.flat_ref, bf16[2,4,288,128]{3,2,1,0:T(8,128)(2,1)} %copy-done.1, bf16[2,4,288,128]{3,2,1,0:T(8,128)(2,1)} %collective-permute-done.8.far_ref, ...), custom_call_target="tpu_custom_call", output_to_operand_aliasing={{0}: (3, {})} | custom-call | tf_op jit(solution)/shard_map/finish/pallas_call | solution.py:425
  (15 shorter events, 4.6 us)
Async XLA Ops:
  3.0 45.3 %collective-permute-start.3 = (bf16[2,4,288,128]{3,2,1,0:T(8,128)(2,1)}, bf16[2,4,288,128]{3,2,1,0:T(8,128)(2,1)}, u32[]{:S(2)}, u32[]{:S(2)}) collective-permute-start(bf16[2,4,288,128]{3,2,1,0:T(8,128)(2,1)} %get-tuple-element.51.refs_0_), channel_id=1, source_target_pairs={{0,1},{1,0},{2,3},{3,2},{4,5},{5,4},{6,7},{7,6},{8,9},{9,8},{10,11... | collective-permute-start | bytes 1769480 | tf_op jit(solution)/shard_map/ppermute | solution.py:528
  6.0 42.2 %collective-permute-start.4 = (bf16[2,4,288,128]{3,2,1,0:T(8,128)(2,1)}, bf16[2,4,288,128]{3,2,1,0:T(8,128)(2,1)}, u32[]{:S(2)}, u32[]{:S(2)}) collective-permute-start(bf16[2,4,288,128]{3,2,1,0:T(8,128)(2,1)} %get-tuple-element.52.refs_1_), channel_id=1, source_target_pairs={{1,2},{2,1},{3,4},{4,3},{5,6},{6,5},{9,10},{10,9},{11,12},{12,11},... | collective-permute-start | bytes 1769480 | tf_op jit(solution)/shard_map/ppermute | solution.py:528
  18.9 51.7 %collective-permute-start.5 = (bf16[2,4,288,128]{3,2,1,0:T(8,128)(2,1)}, bf16[2,4,288,128]{3,2,1,0:T(8,128)(2,1)}, u32[]{:S(2)}, u32[]{:S(2)}) collective-permute-start(bf16[2,4,288,128]{3,2,1,0:T(8,128)(2,1)} %get-tuple-element.61), channel_id=1, source_target_pairs={{0,1},{1,0},{2,3},{3,2},{4,5},{5,4},{6,7},{7,6},{8,9},{9,8},{10,11... | collective-permute-start | bytes 1769480 | tf_op jit(solution)/shard_map/ppermute | solution.py:528
  22.4 48.2 %collective-permute-start.6 = (bf16[2,4,288,128]{3,2,1,0:T(8,128)(2,1)}, bf16[2,4,288,128]{3,2,1,0:T(8,128)(2,1)}, u32[]{:S(2)}, u32[]{:S(2)}) collective-permute-start(bf16[2,4,288,128]{3,2,1,0:T(8,128)(2,1)} %get-tuple-element.62), channel_id=1, source_target_pairs={{1,2},{2,1},{3,4},{4,3},{5,6},{6,5},{9,10},{10,9},{11,12},{12,11},... | collective-permute-start | bytes 1769480 | tf_op jit(solution)/shard_map/ppermute | solution.py:528
  23.9 2.3 %collective-permute-start = (bf16[2,1152,128]{2,1,0:T(8,128)(2,1)}, bf16[2,1152,128]{2,1,0:T(8,128)(2,1)}, u32[]{:S(2)}, u32[]{:S(2)}) collective-permute-start(bf16[2,1152,128]{2,1,0:T(8,128)(2,1)} %get-tuple-element.116), channel_id=1, source_target_pairs={{0,8},{8,0},{16,24},{24,16},{1,9},{9,1},{17,25},{25,17},{2,10},{10... | collective-permute-start | bytes 1769480 | tf_op jit(solution)/shard_map/while/body/ppermute | solution.py:230
  28.3 15.7 %collective-permute-start.1 = (bf16[2,1152,128]{2,1,0:T(8,128)(2,1)}, bf16[2,1152,128]{2,1,0:T(8,128)(2,1)}, u32[]{:S(2)}, u32[]{:S(2)}) collective-permute-start(bf16[2,1152,128]{2,1,0:T(8,128)(2,1)} %add.11.a_ref), channel_id=1, source_target_pairs={{0,16},{8,24},{16,0},{24,8},{1,17},{9,25},{17,1},{25,9},{2,18},{10... | collective-permute-start | bytes 1769480 | tf_op jit(solution)/shard_map/while/body/ppermute | solution.py:233
  45.3 2.1 %collective-permute-start.2 = (bf16[2,1152,128]{2,1,0:T(8,128)(2,1)S(1)}, bf16[2,1152,128]{2,1,0:T(8,128)(2,1)S(1)}, u32[]{:S(2)}, u32[]{:S(2)}) collective-permute-start(bf16[2,1152,128]{2,1,0:T(8,128)(2,1)S(1)} %add.12), channel_id=1, source_target_pairs={{0,8},{8,0},{16,24},{24,16},{1,9},{9,1},{17,25},{25,17},{2,10},{10... | collective-permute-start | bytes 1769480 | tf_op jit(solution)/shard_map/while/body/ppermute | solution.py:235
  47.4 0.8 copy-start
  48.2 47.7 %collective-permute-start.9 = (bf16[2,4,288,128]{3,2,1,0:T(8,128)(2,1)}, bf16[2,4,288,128]{3,2,1,0:T(8,128)(2,1)}, u32[]{:S(2)}, u32[]{:S(2)}) collective-permute-start(bf16[2,4,288,128]{3,2,1,0:T(8,128)(2,1)} %get-tuple-element.59.refs_0_), channel_id=1, source_target_pairs={{0,1},{1,0},{2,3},{3,2},{4,5},{5,4},{6,7},{7,6},{8,9},{9,8},{10,11... | collective-permute-start | bytes 1769480 | tf_op jit(solution)/shard_map/ppermute | solution.py:528
  51.8 44.1 %collective-permute-start.10 = (bf16[2,4,288,128]{3,2,1,0:T(8,128)(2,1)}, bf16[2,4,288,128]{3,2,1,0:T(8,128)(2,1)}, u32[]{:S(2)}, u32[]{:S(2)}) collective-permute-start(bf16[2,4,288,128]{3,2,1,0:T(8,128)(2,1)} %get-tuple-element.60.refs_1_), channel_id=1, source_target_pairs={{1,2},{2,1},{3,4},{4,3},{5,6},{6,5},{9,10},{10,9},{11,12},{12,11},... | collective-permute-start | bytes 1769480 | tf_op jit(solution)/shard_map/ppermute | solution.py:528
  70.6 36.8 %collective-permute-start.7 = (bf16[2,4,288,128]{3,2,1,0:T(8,128)(2,1)}, bf16[2,4,288,128]{3,2,1,0:T(8,128)(2,1)S(1)}, u32[]{:S(2)}, u32[]{:S(2)}) collective-permute-start(bf16[2,4,288,128]{3,2,1,0:T(8,128)(2,1)} %get-tuple-element.69), channel_id=1, source_target_pairs={{0,1},{1,0},{2,3},{3,2},{4,5},{5,4},{6,7},{7,6},{8,9},{9,8},{10,11... | collective-permute-start | bytes 1769480 | tf_op jit(solution)/shard_map/ppermute | solution.py:528
  73.1 34.3 %collective-permute-start.8 = (bf16[2,4,288,128]{3,2,1,0:T(8,128)(2,1)}, bf16[2,4,288,128]{3,2,1,0:T(8,128)(2,1)}, u32[]{:S(2)}, u32[]{:S(2)}) collective-permute-start(bf16[2,4,288,128]{3,2,1,0:T(8,128)(2,1)} %get-tuple-element.70), channel_id=1, source_target_pairs={{1,2},{2,1},{3,4},{4,3},{5,6},{6,5},{9,10},{10,9},{11,12},{12,11},... | collective-permute-start | bytes 1769480 | tf_op jit(solution)/shard_map/ppermute | solution.py:528
  107.4 0.9 copy-start.1

commit v3 on v2

--- a/solution.py
+++ b/solution.py
@@ -419,7 +419,7 @@
         store_rows(parts, i, out_ref)
 
 
-def per_band(body, name, grid, inputs, in_specs, output, out_spec, carry, after, scratch):
+def per_band(body, name, grid, inputs, in_specs, output, out_spec, carry, after, scratch, limit=VMEM_LIMIT):
     anywhere = pl.BlockSpec(memory_space=pl.ANY)
     carried = () if carry is None else (carry,)
     return pl.pallas_call(
@@ -433,7 +433,7 @@
         ],
         input_output_aliases={len(inputs): 0} if carried else {},
         scratch_shapes=scratch,
-        compiler_params=pltpu.CompilerParams(vmem_limit_bytes=VMEM_LIMIT),
+        compiler_params=pltpu.CompilerParams(vmem_limit_bytes=limit),
         cost_estimate=SMALL,
         name=name,
     )(*inputs, *carried, *after)
@@ -492,8 +492,8 @@
     )
 
 
-def finish(flat, near, far, planes, start, carry):
-    count, segment = flat.shape[0], flat.shape[2]
+def finish(flat, near, far, planes, start, skip, carry):
+    count, segment = near.shape[0], flat.shape[2]
     part = segment // 3 if segment % (3 * PACK) == 0 else segment
     halo = pl.BlockSpec((1, 4, part // planes * SUB, LANES), lambda b, i: (b, 0, i, 0))
     return per_band(
@@ -501,17 +501,19 @@
         "finish",
         (count, segment // part),
         (flat, near, far),
-        [pl.BlockSpec((1, 4, part, SUB, LANES), lambda b, i: (b, 0, i, 0, 0)), halo, halo],
+        [pl.BlockSpec((1, 4, part, SUB, LANES), lambda b, i: (skip + b, 0, i, 0, 0)), halo, halo],
         (carry.shape, carry.dtype),
         pl.BlockSpec((1, 4, SUB, part, LANES), lambda b, i: (start + b, 0, 0, i, 0)),
         carry,
         (),
         [],
+        VMEM_LIMIT - 3 * 1024 * 1024,
     )
 
 
 def chunk_sizes(bands):
-    return [2] * (bands // 2) + [1] * (bands % 2)
+    quarter, small = bands // 4, bands // 8
+    return [quarter, bands - 2 * quarter - small, quarter, small] if small else [bands]
 
 
 def shards(spinors, kpt_mult, occupied, core_density, local_potential):
@@ -533,23 +535,17 @@
     halos += [swap(face) for face in faces[1:2]]
     density = group_sum(*density)
     gated = ()
-    if len(starts) > 2:
+    if len(sizes) > 2:
         gated = gate(*faces[2], halos[0] + (density[0],))
         halos.append(swap(gated))
     potential = potential_of(*density, core, local, gated)
-    last = len(starts) - 1
-    out, token, flat = None, (), None
-    for k, start in enumerate(starts):
-        if 0 < k < last - 1:
-            halos.append(swap(gate(*faces[k + 2], halos[k] + token)))
-        if k > 0 and k == last - 1:
-            flat, done = ahead_of(x, potential, planes, starts[last], sizes[last], token)
-            token = (done,)
-        if flat is None or k < last:
-            out, done = apply_bands(x, potential, *halos[k], planes, start, out, token)
-        else:
-            out, done = finish(flat, *halos[k], planes, start, out)
-        token = (done,)
+    out, done = apply_bands(x, potential, *halos[0], planes, 0, None, ())
+    if len(sizes) > 2:
+        flat, done = ahead_of(x, potential, planes, starts[2], sizes[2] + sizes[3], (done,))
+        halos.append(swap(gate(*faces[3], halos[1] + (done,))))
+        out, done = apply_bands(x, potential, *halos[1], planes, starts[1], out, (done,))
+        for k in (2, 3):
+            out, done = finish(flat, *halos[k], planes, starts[k], starts[k] - starts[2], out)
     return planes_view(out.reshape(x.shape), planes)
 
 

time: 115 us -> 114 us (level)
  starting transfers between devices: 20.2 us -> 18.3 us
  transfers between devices with their start and end apart: 11 -> 11, of which waited for: 6 -> 6; matrix products, arithmetic and copies ran while one was open for 0% -> 0% of each run, Pallas kernels for 49% -> 52%
where the time goes in v3:
time: 114 us; the launch traced here: 113 us
  Pallas kernels  65.1 us (57%)
  waiting for transfers between devices  28 us (25%)
  starting transfers between devices  18.3 us (16%)
  local copies, waits for them, and re-layouts  1.62 us (1%)
    pallas_call x5, Pallas kernels, per_band(): pl.pallas_call(body, grid=grid, in_specs=in_specs + [anywhere] * (len(car...  43.5 us
    ppermute x1, waiting for transfers between devices, swaps(): lax.ppermute(turning, 'ka', [(i, (i + 2) % size) for i in range(size)])  14.2 us
    ppermute x4, starting transfers between devices, shards(): lax.ppermute(face[0], 'brick', near_pairs)  11.5 us
    pallas_call x1, Pallas kernels, front(): pl.pallas_call(functools.partial(front_body, planes, 1.0 / (2.0 * total),...  10.9 us
    ppermute x4, waiting for transfers between devices, shards(): lax.ppermute(face[0], 'brick', near_pairs)  9.44 us
    ppermute x4, starting transfers between devices, shards(): lax.ppermute(face[1], 'brick', far_pairs)  5.24 us
    pallas_call x1, Pallas kernels, potential_of(): pl.pallas_call(functools.partial(potential_body, rows), in_specs=[whole]...  4.37 us
    pallas_call x2, Pallas kernels, add(): pl.pallas_call(add_body, in_specs=[whole, whole], out_specs=whole, out_sh...  3.4 us
  transfers between devices with their start and end apart: 11, of which 6 were waited for; matrix products, arithmetic and copies ran while one was open for 0% of the time, Pallas kernels for 52%

profile of v3, /device:TPU:0, one launch (start us, length us, event | category | flops | bytes accessed | tf_op | source)
XLA Modules:
  0.0 113.1 jit_solution(17860234262500669531)
XLA Ops:
  0.0 3.0 %edges.1 = (bf16[2,4,288,128]{3,2,1,0:T(8,128)(2,1)}, bf16[2,4,288,128]{3,2,1,0:T(8,128)(2,1)}) custom-call(bf16[8,4,1152,128]{3,2,1,0:T(8,128)(2,1)} %bitcast.24), custom_call_target="tpu_custom_call" | custom-call | tf_op jit(solution)/shard_map/edges/pallas_call | solution.py:105
  3.0 3.0 %collective-permute-start.3 = (bf16[2,4,288,128]{3,2,1,0:T(8,128)(2,1)}, bf16[2,4,288,128]{3,2,1,0:T(8,128)(2,1)}, u32[]{:S(2)}, u32[]{:S(2)}) collective-permute-start(bf16[2,4,288,128]{3,2,1,0:T(8,128)(2,1)} %get-tuple-element.50.refs_0_), channel_id=1, source_target_pairs={{0,1},{1,0},{2,3},{3,2},{4,5},{5,4},{6,7},{7,6},{8,9},{9,8},{10,11... | collective-permute-start | bytes 1769480 | tf_op jit(solution)/shard_map/ppermute | solution.py:530
  6.0 1.5 %collective-permute-start.4 = (bf16[2,4,288,128]{3,2,1,0:T(8,128)(2,1)}, bf16[2,4,288,128]{3,2,1,0:T(8,128)(2,1)}, u32[]{:S(2)}, u32[]{:S(2)}) collective-permute-start(bf16[2,4,288,128]{3,2,1,0:T(8,128)(2,1)} %get-tuple-element.51.refs_1_), channel_id=1, source_target_pairs={{1,2},{2,1},{3,4},{4,3},{5,6},{6,5},{9,10},{10,9},{11,12},{12,11},... | collective-permute-start | bytes 1769480 | tf_op jit(solution)/shard_map/ppermute | solution.py:530
  7.5 10.9 %front.1 = (bf16[2,8,144,128]{3,2,1,0:T(8,128)(2,1)S(1)}, bf16[2,8,144,128]{3,2,1,0:T(8,128)(2,1)}, bf16[3,4,288,128]{3,2,1,0:T(8,128)(2,1)}, bf16[3,4,288,128]{...) custom-call(s32[8]{0:T(128)} %mult_ref.1, ...), custom_call_target="tpu_custom_call" | custom-call | tf_op jit(solution)/shard_map/front/pallas_call | solution.py:177
  18.4 3.5 %collective-permute-start.5 = (bf16[3,4,288,128]{3,2,1,0:T(8,128)(2,1)}, bf16[3,4,288,128]{3,2,1,0:T(8,128)(2,1)}, u32[]{:S(2)}, u32[]{:S(2)}) collective-permute-start(bf16[3,4,288,128]{3,2,1,0:T(8,128)(2,1)} %get-tuple-element.64), channel_id=1, source_target_pairs={{0,1},{1,0},{2,3},{3,2},{4,5},{5,4},{6,7},{7,6},{8,9},{9,8},{10,11... | collective-permute-start | bytes 2654216 | tf_op jit(solution)/shard_map/ppermute | solution.py:530
  21.9 1.6 %collective-permute-start.6 = (bf16[3,4,288,128]{3,2,1,0:T(8,128)(2,1)}, bf16[3,4,288,128]{3,2,1,0:T(8,128)(2,1)}, u32[]{:S(2)}, u32[]{:S(2)}) collective-permute-start(bf16[3,4,288,128]{3,2,1,0:T(8,128)(2,1)} %get-tuple-element.65), channel_id=1, source_target_pairs={{1,2},{2,1},{3,4},{4,3},{5,6},{6,5},{9,10},{10,9},{11,12},{12,11},... | collective-permute-start | bytes 2654216 | tf_op jit(solution)/shard_map/ppermute | solution.py:530
  23.5 24.3 %while.12 = (s32[]{:T(128)}, bf16[2,1152,128]{2,1,0:T(8,128)(2,1)S(1)}, bf16[2,1152,128]{2,1,0:T(8,128)(2,1)}, s32[]{:T(128)}, s32[]{:T(128)}) while((s32[]{:T(128)}, bf16[2,1152,128]{2,1,0:T(8,128)(2,1)S(1)}, bf16[2,1152,128]{2,1,0:T(8,128)(2,1)}, s32[]{:T(128)}, s32[]{:T(128)}) %tuple.22), condition=%wide.region_1.0_spmd, body=%wide.region_0.0_spmd.sunk | while | flops 2 | bytes 9437393 | solution.py:238
  23.5 2.3 %collective-permute-done.b_ref = bf16[2,1152,128]{2,1,0:T(8,128)(2,1)} collective-permute-done((bf16[2,1152,128]{2,1,0:T(8,128)(2,1)}, bf16[2,1152,128]{2,1,0:T(8,128)(2,1)}, u32[]{:S(2)}, u32[]{:S(2)}) %collective-permute-start) | collective-permute-done | bytes 589856 | tf_op jit(solution)/shard_map/while/body/ppermute | solution.py:230
  25.8 2.0 %add.11.a_ref = bf16[2,1152,128]{2,1,0:T(8,128)(2,1)} custom-call(bf16[2,1152,128]{2,1,0:T(8,128)(2,1)S(1)} %get-tuple-element.113.a_ref, bf16[2,1152,128]{2,1,0:T(8,128)(2,1)} %collective-permute-done.b_ref), custom_call_target="tpu_custom_call" | custom-call | tf_op jit(solution)/shard_map/while/body/add/pallas_call | solution.py:208
  27.9 1.5 %collective-permute-start.1 = (bf16[2,1152,128]{2,1,0:T(8,128)(2,1)}, bf16[2,1152,128]{2,1,0:T(8,128)(2,1)}, u32[]{:S(2)}, u32[]{:S(2)}) collective-permute-start(bf16[2,1152,128]{2,1,0:T(8,128)(2,1)} %add.11.a_ref), channel_id=1, source_target_pairs={{0,16},{8,24},{16,0},{24,8},{1,17},{9,25},{17,1},{25,9},{2,18},{10... | collective-permute-start | bytes 1769480 | tf_op jit(solution)/shard_map/while/body/ppermute | solution.py:233
  29.4 14.2 %collective-permute-done.1.b_ref = bf16[2,1152,128]{2,1,0:T(8,128)(2,1)} collective-permute-done((bf16[2,1152,128]{2,1,0:T(8,128)(2,1)}, bf16[2,1152,128]{2,1,0:T(8,128)(2,1)}, u32[]{:S(2)}, u32[]{:S(2)}) %collective-permute-start.1) | collective-permute-done | bytes 589856 | tf_op jit(solution)/shard_map/while/body/ppermute | solution.py:233
  45.0 2.0 %collective-permute-done.2 = bf16[2,1152,128]{2,1,0:T(8,128)(2,1)S(1)} collective-permute-done((bf16[2,1152,128]{2,1,0:T(8,128)(2,1)S(1)}, bf16[2,1152,128]{2,1,0:T(8,128)(2,1)S(1)}, u32[]{:S(2)}, u32[]{:S(2)}) %collective-permute-start.2) | collective-permute-done | bytes 589856 | tf_op jit(solution)/shard_map/while/body/ppermute | solution.py:235
  47.8 3.8 %collective-permute-done.3.refs_2_.near_ref = bf16[2,4,288,128]{3,2,1,0:T(8,128)(2,1)} collective-permute-done((bf16[2,4,288,128]{3,2,1,0:T(8,128)(2,1)}, bf16[2,4,288,128]{3,2,1,0:T(8,128)(2,1)}, u32[]{:S(2)}, u32[]{:S(2)}) %collective-permute-start.3) | collective-permute-done | bytes 589856 | tf_op jit(solution)/shard_map/ppermute | solution.py:530
  51.6 2.5 %collective-permute-start.9 = (bf16[2,4,288,128]{3,2,1,0:T(8,128)(2,1)}, bf16[2,4,288,128]{3,2,1,0:T(8,128)(2,1)}, u32[]{:S(2)}, u32[]{:S(2)}) collective-permute-start(bf16[2,4,288,128]{3,2,1,0:T(8,128)(2,1)} %get-tuple-element.58.refs_0_), channel_id=1, source_target_pairs={{0,1},{1,0},{2,3},{3,2},{4,5},{5,4},{6,7},{7,6},{8,9},{9,8},{10,11... | collective-permute-start | bytes 1769480 | tf_op jit(solution)/shard_map/ppermute | solution.py:530
  54.1 1.5 %collective-permute-start.10 = (bf16[2,4,288,128]{3,2,1,0:T(8,128)(2,1)}, bf16[2,4,288,128]{3,2,1,0:T(8,128)(2,1)}, u32[]{:S(2)}, u32[]{:S(2)}) collective-permute-start(bf16[2,4,288,128]{3,2,1,0:T(8,128)(2,1)} %get-tuple-element.59.refs_1_), channel_id=1, source_target_pairs={{1,2},{2,1},{3,4},{4,3},{5,6},{6,5},{9,10},{10,9},{11,12},{12,11},... | collective-permute-start | bytes 1769480 | tf_op jit(solution)/shard_map/ppermute | solution.py:530
  55.6 4.4 %potential.1.pot_ref = f32[4,144,8,128]{3,2,1,0:T(8,128)} custom-call(bf16[2,1152,128]{2,1,0:T(8,128)(2,1)S(1)} %get-tuple-element.54.refs_4_.mine_ref, bf16[2,1152,128]{2,1,0:T(8,128)(2,1)} %get-tuple-element.55.other_ref, f32[1152,128]{1,0:T(8,128)} %bitcast.30, f32[1152,128]{1,0:T(8,128)} %bitcast.31, bf16[2,4,288,128]{3,2,1,0:T(8,128)(2,1)} %get-tuple-element.58.refs_0_, ...), custom_call_target="tpu_custom_call" | custom-call | tf_op jit(solution)/shard_map/potential/pallas_call | solution.py:285
  60.0 9.6 %apply.2 = (bf16[8,4,8,144,128]{4,3,2,1,0:T(8,128)(2,1)}, f32[8,128]{1,0:T(8,128)}) custom-call(bf16[8,4,1152,128]{3,2,1,0:T(8,128)(2,1)} %bitcast.26, f32[4,144,8,128]{3,2,1,0:T(8,128)} %potential.1.pot_ref, bf16[2,4,288,128]{3,2,1,0:T(8,128)(2,1)} %collective-permute-done.3.refs_2_.near_ref, bf16[2,4,288,128]{3,2,1,0:T(8,128)(2,1)} %collective-permute-done.4.refs_3_.far_ref), custom_call_target="tpu_custom_call" | custom-call | tf_op jit(solution)/shard_map/apply/pallas_call | solution.py:425
  69.6 11.1 %ahead.1 = (f32[3,4,144,8,128]{4,3,2,1,0:T(8,128)}, f32[8,128]{1,0:T(8,128)}) custom-call(bf16[8,4,1152,128]{3,2,1,0:T(8,128)(2,1)} %bitcast.27, f32[4,144,8,128]{3,2,1,0:T(8,128)} %potential.1.pot_ref, f32[8,128]{1,0:T(8,128)} %get-tuple-element.60.refs_0_), custom_call_target="tpu_custom_call" | custom-call | tf_op jit(solution)/shard_map/ahead/pallas_call | solution.py:425
  80.7 2.6 %collective-permute-done.5.refs_2_.near_ref = bf16[3,4,288,128]{3,2,1,0:T(8,128)(2,1)} collective-permute-done((bf16[3,4,288,128]{3,2,1,0:T(8,128)(2,1)}, bf16[3,4,288,128]{3,2,1,0:T(8,128)(2,1)}, u32[]{:S(2)}, u32[]{:S(2)}) %collective-permute-start.5) | collective-permute-done | bytes 884768 | tf_op jit(solution)/shard_map/ppermute | solution.py:530
  83.2 2.5 %collective-permute-start.7 = (bf16[1,4,288,128]{3,2,1,0:T(8,128)(2,1)}, bf16[1,4,288,128]{3,2,1,0:T(8,128)(2,1)S(1)}, u32[]{:S(2)}, u32[]{:S(2)}) collective-permute-start(bf16[1,4,288,128]{3,2,1,0:T(8,128)(2,1)} %get-tuple-element.67), channel_id=1, source_target_pairs={{0,1},{1,0},{2,3},{3,2},{4,5},{5,4},{6,7},{7,6},{8,9},{9,8},{10,11... | collective-permute-start | bytes 884744 | tf_op jit(solution)/shard_map/ppermute | solution.py:530
  86.4 12.8 %apply.3 = (bf16[8,4,8,144,128]{4,3,2,1,0:T(8,128)(2,1)}, f32[8,128]{1,0:T(8,128)}) custom-call(bf16[8,4,1152,128]{3,2,1,0:T(8,128)(2,1)} %bitcast.28, f32[4,144,8,128]{3,2,1,0:T(8,128)} %potential.1.pot_ref, bf16[3,4,288,128]{3,2,1,0:T(8,128)(2,1)} %collective-permute-done.5.refs_2_.near_ref, ...), custom_call_target="tpu_custom_call", output_to_operand_aliasing={{0}: (4, {})} | custom-call | tf_op jit(solution)/shard_map/apply/pallas_call | solution.py:425
  99.2 3.0 %collective-permute-done.9.near_ref = bf16[2,4,288,128]{3,2,1,0:T(8,128)(2,1)} collective-permute-done((bf16[2,4,288,128]{3,2,1,0:T(8,128)(2,1)}, bf16[2,4,288,128]{3,2,1,0:T(8,128)(2,1)}, u32[]{:S(2)}, u32[]{:S(2)}) %collective-permute-start.9) | collective-permute-done | bytes 589856 | tf_op jit(solution)/shard_map/ppermute | solution.py:530
  102.2 6.2 %finish.2 = (bf16[8,4,8,144,128]{4,3,2,1,0:T(8,128)(2,1)}, f32[8,128]{1,0:T(8,128)}) custom-call(f32[3,4,144,8,128]{4,3,2,1,0:T(8,128)} %get-tuple-element.61.flat_ref, bf16[2,4,288,128]{3,2,1,0:T(8,128)(2,1)} %collective-permute-done.9.near_ref, bf16[2,4,288,128]{3,2,1,0:T(8,128)(2,1)} %collective-permute-done.10.far_ref, ...), custom_call_target="tpu_custom_call", output_to_operand_aliasing={{0}: (3, {})} | custom-call | tf_op jit(solution)/shard_map/finish/pallas_call | solution.py:425
  109.2 3.9 %finish.3 = (bf16[8,4,8,144,128]{4,3,2,1,0:T(8,128)(2,1)}, f32[8,128]{1,0:T(8,128)}) custom-call(f32[3,4,144,8,128]{4,3,2,1,0:T(8,128)} %get-tuple-element.61.flat_ref, bf16[1,4,288,128]{3,2,1,0:T(8,128)(2,1)} %copy-done.1, bf16[1,4,288,128]{3,2,1,0:T(8,128)(2,1)} %copy-done.2, ...), custom_call_target="tpu_custom_call", output_to_operand_aliasing={{0}: (3, {})} | custom-call | tf_op jit(solution)/shard_map/finish/pallas_call | solution.py:425
  (17 shorter events, 3.8 us)
Async XLA Ops:
  3.0 48.7 %collective-permute-start.3 = (bf16[2,4,288,128]{3,2,1,0:T(8,128)(2,1)}, bf16[2,4,288,128]{3,2,1,0:T(8,128)(2,1)}, u32[]{:S(2)}, u32[]{:S(2)}) collective-permute-start(bf16[2,4,288,128]{3,2,1,0:T(8,128)(2,1)} %get-tuple-element.50.refs_0_), channel_id=1, source_target_pairs={{0,1},{1,0},{2,3},{3,2},{4,5},{5,4},{6,7},{7,6},{8,9},{9,8},{10,11... | collective-permute-start | bytes 1769480 | tf_op jit(solution)/shard_map/ppermute | solution.py:530
  6.0 45.7 %collective-permute-start.4 = (bf16[2,4,288,128]{3,2,1,0:T(8,128)(2,1)}, bf16[2,4,288,128]{3,2,1,0:T(8,128)(2,1)}, u32[]{:S(2)}, u32[]{:S(2)}) collective-permute-start(bf16[2,4,288,128]{3,2,1,0:T(8,128)(2,1)} %get-tuple-element.51.refs_1_), channel_id=1, source_target_pairs={{1,2},{2,1},{3,4},{4,3},{5,6},{6,5},{9,10},{10,9},{11,12},{12,11},... | collective-permute-start | bytes 1769480 | tf_op jit(solution)/shard_map/ppermute | solution.py:530
  18.4 64.8 %collective-permute-start.5 = (bf16[3,4,288,128]{3,2,1,0:T(8,128)(2,1)}, bf16[3,4,288,128]{3,2,1,0:T(8,128)(2,1)}, u32[]{:S(2)}, u32[]{:S(2)}) collective-permute-start(bf16[3,4,288,128]{3,2,1,0:T(8,128)(2,1)} %get-tuple-element.64), channel_id=1, source_target_pairs={{0,1},{1,0},{2,3},{3,2},{4,5},{5,4},{6,7},{7,6},{8,9},{9,8},{10,11... | collective-permute-start | bytes 2654216 | tf_op jit(solution)/shard_map/ppermute | solution.py:530
  21.9 61.3 %collective-permute-start.6 = (bf16[3,4,288,128]{3,2,1,0:T(8,128)(2,1)}, bf16[3,4,288,128]{3,2,1,0:T(8,128)(2,1)}, u32[]{:S(2)}, u32[]{:S(2)}) collective-permute-start(bf16[3,4,288,128]{3,2,1,0:T(8,128)(2,1)} %get-tuple-element.65), channel_id=1, source_target_pairs={{1,2},{2,1},{3,4},{4,3},{5,6},{6,5},{9,10},{10,9},{11,12},{12,11},... | collective-permute-start | bytes 2654216 | tf_op jit(solution)/shard_map/ppermute | solution.py:530
  23.5 2.3 %collective-permute-start = (bf16[2,1152,128]{2,1,0:T(8,128)(2,1)}, bf16[2,1152,128]{2,1,0:T(8,128)(2,1)}, u32[]{:S(2)}, u32[]{:S(2)}) collective-permute-start(bf16[2,1152,128]{2,1,0:T(8,128)(2,1)} %get-tuple-element.114), channel_id=1, source_target_pairs={{0,8},{8,0},{16,24},{24,16},{1,9},{9,1},{17,25},{25,17},{2,10},{10... | collective-permute-start | bytes 1769480 | tf_op jit(solution)/shard_map/while/body/ppermute | solution.py:230
  27.9 15.7 %collective-permute-start.1 = (bf16[2,1152,128]{2,1,0:T(8,128)(2,1)}, bf16[2,1152,128]{2,1,0:T(8,128)(2,1)}, u32[]{:S(2)}, u32[]{:S(2)}) collective-permute-start(bf16[2,1152,128]{2,1,0:T(8,128)(2,1)} %add.11.a_ref), channel_id=1, source_target_pairs={{0,16},{8,24},{16,0},{24,8},{1,17},{9,25},{17,1},{25,9},{2,18},{10... | collective-permute-start | bytes 1769480 | tf_op jit(solution)/shard_map/while/body/ppermute | solution.py:233
  44.9 2.1 %collective-permute-start.2 = (bf16[2,1152,128]{2,1,0:T(8,128)(2,1)S(1)}, bf16[2,1152,128]{2,1,0:T(8,128)(2,1)S(1)}, u32[]{:S(2)}, u32[]{:S(2)}) collective-permute-start(bf16[2,1152,128]{2,1,0:T(8,128)(2,1)S(1)} %add.12), channel_id=1, source_target_pairs={{0,8},{8,0},{16,24},{24,16},{1,9},{9,1},{17,25},{25,17},{2,10},{10... | collective-permute-start | bytes 1769480 | tf_op jit(solution)/shard_map/while/body/ppermute | solution.py:235
  47.0 0.8 copy-start
  51.6 50.6 %collective-permute-start.9 = (bf16[2,4,288,128]{3,2,1,0:T(8,128)(2,1)}, bf16[2,4,288,128]{3,2,1,0:T(8,128)(2,1)}, u32[]{:S(2)}, u32[]{:S(2)}) collective-permute-start(bf16[2,4,288,128]{3,2,1,0:T(8,128)(2,1)} %get-tuple-element.58.refs_0_), channel_id=1, source_target_pairs={{0,1},{1,0},{2,3},{3,2},{4,5},{5,4},{6,7},{7,6},{8,9},{9,8},{10,11... | collective-permute-start | bytes 1769480 | tf_op jit(solution)/shard_map/ppermute | solution.py:530
  54.1 48.1 %collective-permute-start.10 = (bf16[2,4,288,128]{3,2,1,0:T(8,128)(2,1)}, bf16[2,4,288,128]{3,2,1,0:T(8,128)(2,1)}, u32[]{:S(2)}, u32[]{:S(2)}) collective-permute-start(bf16[2,4,288,128]{3,2,1,0:T(8,128)(2,1)} %get-tuple-element.59.refs_1_), channel_id=1, source_target_pairs={{1,2},{2,1},{3,4},{4,3},{5,6},{6,5},{9,10},{10,9},{11,12},{12,11},... | collective-permute-start | bytes 1769480 | tf_op jit(solution)/shard_map/ppermute | solution.py:530
  83.2 25.1 %collective-permute-start.7 = (bf16[1,4,288,128]{3,2,1,0:T(8,128)(2,1)}, bf16[1,4,288,128]{3,2,1,0:T(8,128)(2,1)S(1)}, u32[]{:S(2)}, u32[]{:S(2)}) collective-permute-start(bf16[1,4,288,128]{3,2,1,0:T(8,128)(2,1)} %get-tuple-element.67), channel_id=1, source_target_pairs={{0,1},{1,0},{2,3},{3,2},{4,5},{5,4},{6,7},{7,6},{8,9},{9,8},{10,11... | collective-permute-start | bytes 884744 | tf_op jit(solution)/shard_map/ppermute | solution.py:530
  85.7 22.7 %collective-permute-start.8 = (bf16[1,4,288,128]{3,2,1,0:T(8,128)(2,1)}, bf16[1,4,288,128]{3,2,1,0:T(8,128)(2,1)S(1)}, u32[]{:S(2)}, u32[]{:S(2)}) collective-permute-start(bf16[1,4,288,128]{3,2,1,0:T(8,128)(2,1)} %get-tuple-element.68), channel_id=1, source_target_pairs={{1,2},{2,1},{3,4},{4,3},{5,6},{6,5},{9,10},{10,9},{11,12},{12,11},... | collective-permute-start | bytes 884744 | tf_op jit(solution)/shard_map/ppermute | solution.py:530
  108.4 0.7 copy-start.1
  108.4 0.8 copy-start.2
